TPU v7x, 32 devices: a whole 2x2x4 slice. The times are simulated.
32 devices in a mesh: tm: 4 (over y, x), tile: 8 (over z, core).
Axes of the slice: x: 2, y: 2, z: 4, core: 2. Of those that a mesh axis runs over, the one named last changes fastest.
Arguments:
- latent: bfloat16 [16, 32, 32, 256], P('tm', 'tile'), may hold values from -6 to 6
- tile_rows: int32 [8], replicated, may hold values from 1 to 4, 16 in all
- kernel_one: bfloat16 [3, 3, 3, 256, 256], replicated, may hold values from -0.078125 to 0.078125
- bias_one: float32 [256], replicated, may hold values from -3 to 3
- kernel_two: bfloat16 [3, 3, 3, 256, 256], replicated, may hold values from -0.078125 to 0.078125
- bias_two: float32 [256], replicated, may hold values from -3 to 3
Outputs:
- frames_out: bfloat16 [16, 64, 64, 256], P('tm', 'tile')
Inputs may be any that keep to these rules, and one draw needn't show every extreme that they name: `tile_rows`: each tile has 1 to 4 rows, they sum to 16, and some tile has exactly 4.
All inputs are finite; a program needn't handle non-finite values.
Results may differ from a plain program's by a relative error of at most 0.0031.
Values may be sent and summed in bfloat16 or wider, within the bound.
No kernel may reach another device: no remote copies, remote signals or barrier semaphores. Data moves between devices by JAX's collectives and lax.ppermute only.
A program may use at most 64 MiB of HBM per device.

v0:
```python
import jax
import jax.numpy as jnp
from jax import lax
from jax.sharding import PartitionSpec as P


def padded(block, sides, width):
    for axis, dim in sides:
        count = lax.axis_size(axis)
        forward = [(i, i + 1) for i in range(count - 1)]
        backward = [(target, source) for source, target in forward]
        low = lax.ppermute(
            lax.slice_in_dim(block, block.shape[dim] - width, None, axis=dim), axis, forward
        )
        high = lax.ppermute(lax.slice_in_dim(block, 0, width, axis=dim), axis, backward)
        block = jnp.concatenate([low, block, high], axis=dim)
    return block


def passed_along(block, axis, distance):
    devices = range(lax.axis_size(axis))
    route = [(i - distance, i) for i in devices if i - distance in devices]
    return lax.ppermute(block, axis, route)


def upsample(field):
    return jnp.repeat(jnp.repeat(field, 2, axis=1), 2, axis=2)


def edge_pair(field, last):
    tail = lax.dynamic_slice_in_dim(field, last, 1, axis=1)
    return jnp.concatenate([field[:, 0:1], tail], axis=1)


def attach(field, above, below, place):
    extended = jnp.concatenate([above, field, jnp.zeros_like(above)], axis=1)
    row_ids = jnp.arange(extended.shape[1], dtype=jnp.int32)
    return jnp.where((row_ids == place)[None, :, None, None], below, extended)


def convolve(field, kernel, bias):
    result = lax.conv_general_dilated(
        field[None],
        kernel,
        (1, 1, 1),
        ((0, 0), (0, 0), (1, 1)),
        dimension_numbers=("NDHWC", "DHWIO", "NDHWC"),
        preferred_element_type=jnp.float32,
    )
    return result[0] + bias


def local(latent, tile_rows, kernel_one, bias_one, kernel_two, bias_two):
    frames = latent.shape[0]
    cap = latent.shape[1]
    tile_pos = lax.axis_index("tile")
    length = lax.dynamic_slice_in_dim(tile_rows, tile_pos, 1)[0]
    first_group = lax.axis_index("tm") == 0
    valid = jnp.arange(cap, dtype=jnp.int32) < length
    clean = jnp.where(valid[None, :, None, None], latent, 0)
    rimmed = padded(edge_pair(clean, length - 1), (("tile", 1),), 1)
    lat_ext = attach(clean, rimmed[:, 0:1], rimmed[:, 3:4], length + 1)
    residual = upsample(clean).astype(jnp.float32)
    earlier = passed_along(lat_ext[frames - 2 :], "tm", 1)
    earlier = jnp.where(first_group, jnp.broadcast_to(lat_ext[0:1], earlier.shape), earlier)
    source = upsample(jnp.concatenate([earlier, lat_ext], axis=0))[:, 1 : 2 * cap + 3]
    act_one = convolve(source, kernel_one, bias_one)
    keep = jnp.arange(2 * cap, dtype=jnp.int32) < 2 * length
    hidden = jnp.where(keep[None, :, None, None], jax.nn.silu(act_one), 0.0).astype(jnp.bfloat16)
    rimmed_hidden = padded(edge_pair(hidden, 2 * length - 1), (("tile", 1),), 1)
    own = attach(hidden, rimmed_hidden[:, 0:1], rimmed_hidden[:, 3:4], 2 * length + 1)
    before = passed_along(own[frames - 2 :], "tm", 1)
    before = jnp.where(first_group, jnp.broadcast_to(own[0:1], before.shape), before)
    hid_ext = jnp.concatenate([before, own], axis=0)
    act_two = convolve(hid_ext, kernel_two, bias_two)
    out_keep = jnp.arange(2 * cap, dtype=jnp.int32) < 2 * length
    return jnp.where(out_keep[None, :, None, None], act_two + residual, 0.0).astype(jnp.bfloat16)


def solution(mesh):
    in_specs = (P("tm", "tile", None, None), P(), P(), P(), P(), P())
    out_specs = P("tm", "tile", None, None)
    return jax.shard_map(local, mesh=mesh, in_specs=in_specs, out_specs=out_specs, check_vma=False)
```

profile of v0, /device:TPU:12, one launch (start us, length us, event | category | flops | bytes accessed | tf_op | source)
XLA Modules:
  0.0 89.4 jit_solution(9832113877072393553)
XLA Ops:
  0.0 1.4 %dynamic_slice.9 = s32[1]{0:T(128)} dynamic-slice(s32[8]{0:T(128)} %param.7, s32[]{:T(128)S(6)} %select_n.44), dynamic_slice_sizes={1} | dynamic-slice | bytes 12 | tf_op jit(solution)/shard_map/dynamic_slice | solution.py:57
  5.7 1.9 %collective-permute-start = (bf16[4,1,32,256]{3,2,1,0:T(8,128)(2,1)}, bf16[4,1,32,256]{3,2,1,0:T(8,128)(2,1)}, u32[]{:S(2)}, u32[]{:S(2)}) collective-permute-start(bf16[4,1,32,256]{3,2,1,0:T(8,128)(2,1)} %get-tuple-element.7), channel_id=1, source_target_pairs={{1,0},{2,1},{3,2},{4,3},{5,4},{6,5},{7,6},{9,8},{10,9},{11,10},{12... | collective-permute-start | bytes 196616 | tf_op jit(solution)/shard_map/ppermute | solution.py:15
  7.6 2.4 %collective-permute-start.1 = (bf16[4,1,32,256]{3,2,1,0:T(8,128)(2,1)}, bf16[4,1,32,256]{3,2,1,0:T(8,128)(2,1)}, u32[]{:S(2)}, u32[]{:S(2)}) collective-permute-start(bf16[4,1,32,256]{3,2,1,0:T(8,128)(2,1)} %get-tuple-element.8), channel_id=1, source_target_pairs={{0,1},{1,2},{2,3},{3,4},{4,5},{5,6},{6,7},{8,9},{9,10},{10,11},{11... | collective-permute-start | bytes 196616 | tf_op jit(solution)/shard_map/ppermute | solution.py:12
  11.3 2.2 %collective-permute-done.1 = bf16[4,1,32,256]{3,2,1,0:T(8,128)(2,1)} collective-permute-done((bf16[4,1,32,256]{3,2,1,0:T(8,128)(2,1)}, bf16[4,1,32,256]{3,2,1,0:T(8,128)(2,1)}, u32[]{:S(2)}, u32[]{:S(2)}) %collective-permute-start.1) | collective-permute-done | bytes 65568 | tf_op jit(solution)/shard_map/ppermute | solution.py:12
  13.5 1.1 %maximum_select_fusion.1 = bf16[4,6,32,256]{3,2,1,0:T(8,128)(2,1)S(1)} fusion(bf16[4,4,32,256]{3,2,1,0:T(8,128)(2,1)} %copy-done.5, bf16[4,1,32,256]{3,2,1,0:T(8,128)(2,1)} %collective-permute-done.1, pred[6]{0:T(512)(128)(4,1)S(1)} %iota_compare_fusion.2, bf16[6]{0:T(256)(128)(2,1)S(1)} %pad.17.clone, bf16[4,32,256]{2,1,0:T(8,128)(2,1)} %bitcast.1), kind=kLoop, calls=%fused_computation.33 | loop fusion | flops 589824 | bytes 786450 | tf_op jit(solution)/shard_map/jit(_where)/select_n | solution.py:38
  14.6 3.4 %collective-permute-start.2 = (bf16[2,6,32,256]{3,2,1,0:T(8,128)(2,1)S(1)}, bf16[2,6,32,256]{3,2,1,0:T(8,128)(2,1)S(1)}, u32[]{:S(2)}, u32[]{:S(2)}) collective-permute-start(bf16[2,6,32,256]{3,2,1,0:T(8,128)(2,1)S(1)} %slice.34), channel_id=1, source_target_pairs={{0,8},{8,16},{16,24},{1,9},{9,17},{17,25},{2,10},{10,18},{18,26},{... | collective-permute-start | bytes 589832 | tf_op jit(solution)/shard_map/ppermute | solution.py:23
  18.0 5.5 %collective-permute-done.2 = bf16[2,6,32,256]{3,2,1,0:T(8,128)(2,1)S(1)} collective-permute-done((bf16[2,6,32,256]{3,2,1,0:T(8,128)(2,1)S(1)}, bf16[2,6,32,256]{3,2,1,0:T(8,128)(2,1)S(1)}, u32[]{:S(2)}, u32[]{:S(2)}) %collective-permute-start.2) | collective-permute-done | bytes 196640 | tf_op jit(solution)/shard_map/ppermute | solution.py:23
  25.7 9.0 %fusion.24 = f32[4,8,8,9,256]{4,2,3,1,0:T(8,128)S(1)} fusion(bf16[3,3,3,256,256]{4,3,2,1,0:T(8,128)(2,1)S(1)} %copy-done, bf16[6,10,1,7,2,256]{5,3,4,1,0,2:T(8,128)(2,1)S(1)} %slice.36, bf16[6,10,1,8,9,256]{5,3,4,1,0,2:T(8,128)(2,1)S(1)} %copy.29, pred[8,9]{0,1:T(8,128)(4,1)S(1)} %copy-done.10), kind=kOutput, calls=%fused_computation.27 | convolution fusion | flops 8162426880 | bytes 8540232 | tf_op jit(solution)/shard_map/conv_general_dilated | solution.py:42
  37.3 1.2 %fusion.35 = (bf16[4,1,64,256]{3,1,2,0:T(2,128)(2,1)}, bf16[4,1,64,256]{3,1,2,0:T(2,128)(2,1)}) fusion(bf16[4,8,64,256]{3,1,2,0:T(8,128)(2,1)S(1)} %select_convert_fusion, s32[]{:T(128)S(6)} %select_n.52), kind=kLoop, calls=%fused_computation.50 | loop fusion | bytes 524292 | tf_op jit(solution)/shard_map/slice | solution.py:32
  38.5 2.0 %collective-permute-start.3 = (bf16[4,1,64,256]{3,1,2,0:T(2,128)(2,1)}, bf16[4,1,64,256]{3,1,2,0:T(2,128)(2,1)}, u32[]{:S(2)}, u32[]{:S(2)}) collective-permute-start(bf16[4,1,64,256]{3,1,2,0:T(2,128)(2,1)} %get-tuple-element.5), channel_id=1, source_target_pairs={{1,0},{2,1},{3,2},{4,3},{5,4},{6,5},{7,6},{9,8},{10,9},{11,10},{12... | collective-permute-start | bytes 393224 | tf_op jit(solution)/shard_map/ppermute | solution.py:15
  40.5 2.4 %collective-permute-start.4 = (bf16[4,1,64,256]{3,1,2,0:T(2,128)(2,1)}, bf16[4,1,64,256]{3,1,2,0:T(2,128)(2,1)}, u32[]{:S(2)}, u32[]{:S(2)}) collective-permute-start(bf16[4,1,64,256]{3,1,2,0:T(2,128)(2,1)} %get-tuple-element.6), channel_id=1, source_target_pairs={{0,1},{1,2},{2,3},{3,4},{4,5},{5,6},{6,7},{8,9},{9,10},{10,11},{11... | collective-permute-start | bytes 393224 | tf_op jit(solution)/shard_map/ppermute | solution.py:12
  42.9 1.7 %collective-permute-done.3 = bf16[4,1,64,256]{3,1,2,0:T(2,128)(2,1)} collective-permute-done((bf16[4,1,64,256]{3,1,2,0:T(2,128)(2,1)}, bf16[4,1,64,256]{3,1,2,0:T(2,128)(2,1)}, u32[]{:S(2)}, u32[]{:S(2)}) %collective-permute-start.3) | collective-permute-done | bytes 131104 | tf_op jit(solution)/shard_map/ppermute | solution.py:15
  45.6 2.9 %collective-permute-done.4 = bf16[4,1,64,256]{3,1,2,0:T(2,128)(2,1)} collective-permute-done((bf16[4,1,64,256]{3,1,2,0:T(2,128)(2,1)}, bf16[4,1,64,256]{3,1,2,0:T(2,128)(2,1)}, u32[]{:S(2)}, u32[]{:S(2)}) %collective-permute-start.4) | collective-permute-done | bytes 131104 | tf_op jit(solution)/shard_map/ppermute | solution.py:12
  48.5 2.7 %maximum_select_fusion = bf16[4,10,64,256]{3,1,2,0:T(8,128)(2,1)S(1)} fusion(bf16[4,8,64,256]{3,1,2,0:T(8,128)(2,1)} %copy-done.3, bf16[4,1,64,256]{3,1,2,0:T(2,128)(2,1)} %collective-permute-done.4, pred[10]{0:T(512)(128)(4,1)S(1)} %iota_compare_fusion.3, bf16[10]{0:T(256)(128)(2,1)S(1)} %pad.10.clone, bf16[4,64,256]{2,1,0:T(8,128)(2,1)S(1)} %bitcast.59), kind=kLoop, calls=%fused_computation.24 | loop fusion | flops 4587520 | bytes 2621470 | tf_op jit(solution)/shard_map/jit(_where)/select_n | solution.py:38
  51.2 1.3 %copy-done.1 = bf16[4,10,64,256]{3,1,2,0:T(8,128)(2,1)} copy-done((bf16[4,10,64,256]{3,1,2,0:T(8,128)(2,1)}, bf16[4,10,64,256]{3,1,2,0:T(8,128)(2,1)S(1)}, u32[]{:S(2)}) %copy-start.1) | copy-done | bytes 1310744
  52.6 1.1 %copy.31 = bf16[2,10,64,256]{3,2,1,0:T(8,128)(2,1)} copy(bf16[2,10,64,256]{3,1,2,0:T(8,128)(2,1)S(1)} %slice.40) | data formatting | bytes 1310720 | tf_op jit(solution)/shard_map/slice | solution.py:72
  53.7 2.5 %collective-permute-start.5 = (bf16[2,10,64,256]{3,2,1,0:T(8,128)(2,1)}, bf16[2,10,64,256]{3,2,1,0:T(8,128)(2,1)}, u32[]{:S(2)}, u32[]{:S(2)}) collective-permute-start(bf16[2,10,64,256]{3,2,1,0:T(8,128)(2,1)} %copy.31), channel_id=1, source_target_pairs={{0,8},{8,16},{16,24},{1,9},{9,17},{17,25},{2,10},{10,18},{18,26},{... | collective-permute-start | bytes 1966088 | tf_op jit(solution)/shard_map/ppermute | solution.py:23
  56.4 1.3 %broadcast_in_dim.129 = f32[4,4,2,32,256]{4,2,1,3,0:T(2,128)} broadcast(f32[4,4,32,256]{3,1,2,0:T(4,128)S(1)} %copy.37), dimensions={0,1,3,4} | broadcast | bytes 1572864 | tf_op jit(solution)/shard_map/broadcast_in_dim | solution.py:27
  57.7 2.9 %convert_element_type.21 = f32[4,8,32,256]{3,1,2,0:T(8,128)} reshape(f32[4,4,2,32,256]{4,2,1,3,0:T(2,128)} %broadcast_in_dim.129) | data formatting | bytes 2097152 | tf_op jit(solution)/shard_map/convert_element_type | solution.py:63
  60.6 1.2 %slice_bitcast_fusion.3 = bf16[10,64,256]{2,0,1:T(8,128)(2,1)S(1)} fusion(bf16[4,10,64,256]{3,1,2,0:T(8,128)(2,1)} %copy-done.1), kind=kLoop, calls=%fused_computation.32 | loop fusion | bytes 655360 | tf_op jit(solution)/shard_map/broadcast_in_dim | solution.py:73
  61.9 10.8 %collective-permute-done.5 = bf16[2,10,64,256]{3,2,1,0:T(8,128)(2,1)} collective-permute-done((bf16[2,10,64,256]{3,2,1,0:T(8,128)(2,1)}, bf16[2,10,64,256]{3,2,1,0:T(8,128)(2,1)}, u32[]{:S(2)}, u32[]{:S(2)}) %collective-permute-start.5) | collective-permute-done | bytes 655392 | tf_op jit(solution)/shard_map/ppermute | solution.py:23
  72.7 1.5 %copy_select_fusion = bf16[2,10,64,256]{3,1,2,0:T(8,128)(2,1)S(1)} fusion(bf16[2,10,64,256]{3,2,1,0:T(8,128)(2,1)} %collective-permute-done.5, pred[]{:T(512)S(6)} %eq.23, bf16[10,64,256]{2,0,1:T(8,128)(2,1)S(1)} %slice_bitcast_fusion.3), kind=kLoop, calls=%fused_computation.30 | loop fusion | flops 327680 | bytes 1638401 | tf_op jit(solution)/shard_map/jit(_where)/select_n | solution.py:73
  77.1 9.1 %fusion.21 = f32[4,8,8,9,256]{4,2,3,1,0:T(8,128)S(1)} fusion(bf16[3,3,3,256,256]{4,3,2,1,0:T(8,128)(2,1)S(1)} %copy-done.9, bf16[6,10,1,7,2,256]{5,3,4,1,0,2:T(8,128)(2,1)S(1)} %slice.41, bf16[6,10,1,8,9,256]{5,3,4,1,0,2:T(8,128)(2,1)S(1)} %copy.35, pred[8,9]{0,1:T(8,128)(4,1)S(1)} %copy-done.10), kind=kOutput, calls=%fused_computation.26 | convolution fusion | flops 8162426880 | bytes 8540232 | tf_op jit(solution)/shard_map/conv_general_dilated | solution.py:42
  88.1 1.2 %copy.38 = bf16[4,8,64,256]{3,2,1,0:T(8,128)(2,1)} copy(bf16[4,8,64,256]{3,1,2,0:T(8,128)(2,1)S(1)} %fusion.19) | data formatting | bytes 2097152 | tf_op jit(solution)/shard_map/convert_element_type | solution.py:77
  (53 shorter events, 13.9 us)
Async XLA Ops:
  0.0 25.6 %copy-start = (bf16[3,3,3,256,256]{4,3,2,1,0:T(8,128)(2,1)S(1)}, bf16[3,3,3,256,256]{4,3,2,1,0:T(8,128)(2,1)}, u32[]{:S(2)}) copy-start(bf16[3,3,3,256,256]{4,3,2,1,0:T(8,128)(2,1)} %param.8) | copy-start | bytes 10616836
  4.3 0.7 copy-start.5
  5.7 5.7 %collective-permute-start = (bf16[4,1,32,256]{3,2,1,0:T(8,128)(2,1)}, bf16[4,1,32,256]{3,2,1,0:T(8,128)(2,1)}, u32[]{:S(2)}, u32[]{:S(2)}) collective-permute-start(bf16[4,1,32,256]{3,2,1,0:T(8,128)(2,1)} %get-tuple-element.7), channel_id=1, source_target_pairs={{1,0},{2,1},{3,2},{4,3},{5,4},{6,5},{7,6},{9,8},{10,9},{11,10},{12... | collective-permute-start | bytes 196616 | tf_op jit(solution)/shard_map/ppermute | solution.py:15
  7.6 5.9 %collective-permute-start.1 = (bf16[4,1,32,256]{3,2,1,0:T(8,128)(2,1)}, bf16[4,1,32,256]{3,2,1,0:T(8,128)(2,1)}, u32[]{:S(2)}, u32[]{:S(2)}) collective-permute-start(bf16[4,1,32,256]{3,2,1,0:T(8,128)(2,1)} %get-tuple-element.8), channel_id=1, source_target_pairs={{0,1},{1,2},{2,3},{3,4},{4,5},{5,6},{6,7},{8,9},{9,10},{10,11},{11... | collective-permute-start | bytes 196616 | tf_op jit(solution)/shard_map/ppermute | solution.py:12
  14.6 8.9 %collective-permute-start.2 = (bf16[2,6,32,256]{3,2,1,0:T(8,128)(2,1)S(1)}, bf16[2,6,32,256]{3,2,1,0:T(8,128)(2,1)S(1)}, u32[]{:S(2)}, u32[]{:S(2)}) collective-permute-start(bf16[2,6,32,256]{3,2,1,0:T(8,128)(2,1)S(1)} %slice.34), channel_id=1, source_target_pairs={{0,8},{8,16},{16,24},{1,9},{9,17},{17,25},{2,10},{10,18},{18,26},{... | collective-permute-start | bytes 589832 | tf_op jit(solution)/shard_map/ppermute | solution.py:23
  25.1 0.7 copy-start.10
  34.8 0.7 copy-start.7
  36.3 1.0 %copy-start.3 = (bf16[4,8,64,256]{3,1,2,0:T(8,128)(2,1)}, bf16[4,8,64,256]{3,1,2,0:T(8,128)(2,1)S(1)}, u32[]{:S(2)}) copy-start(bf16[4,8,64,256]{3,1,2,0:T(8,128)(2,1)S(1)} %select_convert_fusion) | copy-start | bytes 3145732
  38.5 6.1 %collective-permute-start.3 = (bf16[4,1,64,256]{3,1,2,0:T(2,128)(2,1)}, bf16[4,1,64,256]{3,1,2,0:T(2,128)(2,1)}, u32[]{:S(2)}, u32[]{:S(2)}) collective-permute-start(bf16[4,1,64,256]{3,1,2,0:T(2,128)(2,1)} %get-tuple-element.5), channel_id=1, source_target_pairs={{1,0},{2,1},{3,2},{4,3},{5,4},{6,5},{7,6},{9,8},{10,9},{11,10},{12... | collective-permute-start | bytes 393224 | tf_op jit(solution)/shard_map/ppermute | solution.py:15
  40.5 8.0 %collective-permute-start.4 = (bf16[4,1,64,256]{3,1,2,0:T(2,128)(2,1)}, bf16[4,1,64,256]{3,1,2,0:T(2,128)(2,1)}, u32[]{:S(2)}, u32[]{:S(2)}) collective-permute-start(bf16[4,1,64,256]{3,1,2,0:T(2,128)(2,1)} %get-tuple-element.6), channel_id=1, source_target_pairs={{0,1},{1,2},{2,3},{3,4},{4,5},{5,6},{6,7},{8,9},{9,10},{10,11},{11... | collective-permute-start | bytes 393224 | tf_op jit(solution)/shard_map/ppermute | solution.py:12
  51.2 1.3 %copy-start.1 = (bf16[4,10,64,256]{3,1,2,0:T(8,128)(2,1)}, bf16[4,10,64,256]{3,1,2,0:T(8,128)(2,1)S(1)}, u32[]{:S(2)}) copy-start(bf16[4,10,64,256]{3,1,2,0:T(8,128)(2,1)S(1)} %maximum_select_fusion) | copy-start | bytes 3932164
  52.5 3.6 %copy-start.6 = (bf16[4,4,32,256]{3,2,1,0:T(8,128)(2,1)S(1)}, bf16[4,4,32,256]{3,2,1,0:T(8,128)(2,1)}, u32[]{:S(2)}) copy-start(bf16[4,4,32,256]{3,2,1,0:T(8,128)(2,1)} %copy-done.5) | copy-start | bytes 786436
  53.7 19.0 %collective-permute-start.5 = (bf16[2,10,64,256]{3,2,1,0:T(8,128)(2,1)}, bf16[2,10,64,256]{3,2,1,0:T(8,128)(2,1)}, u32[]{:S(2)}, u32[]{:S(2)}) collective-permute-start(bf16[2,10,64,256]{3,2,1,0:T(8,128)(2,1)} %copy.31), channel_id=1, source_target_pairs={{0,8},{8,16},{16,24},{1,9},{9,17},{17,25},{2,10},{10,18},{18,26},{... | collective-permute-start | bytes 1966088 | tf_op jit(solution)/shard_map/ppermute | solution.py:23
  60.6 13.5 %copy-start.2 = (bf16[4,10,64,256]{3,1,2,0:T(8,128)(2,1)S(1)}, bf16[4,10,64,256]{3,1,2,0:T(8,128)(2,1)}, u32[]{:S(2)}) copy-start(bf16[4,10,64,256]{3,1,2,0:T(8,128)(2,1)} %copy-done.1) | copy-start | bytes 3932164
  75.0 2.0 %copy-start.9 = (bf16[3,3,3,256,256]{4,3,2,1,0:T(8,128)(2,1)S(1)}, bf16[3,3,3,256,256]{4,3,2,1,0:T(8,128)(2,1)}, u32[]{:S(2)}) copy-start(bf16[3,3,3,256,256]{4,3,2,1,0:T(8,128)(2,1)} %param.10) | copy-start | bytes 10616836
  86.1 1.2 %copy-start.4 = (f32[4,8,32,256]{3,1,2,0:T(8,128)S(1)}, f32[4,8,32,256]{3,1,2,0:T(8,128)}, u32[]{:S(2)}) copy-start(f32[4,8,32,256]{3,1,2,0:T(8,128)} %convert_element_type.21) | copy-start | bytes 3145732
  86.9 0.8 copy-start.8
where the time goes:
time: 89.9 us; the launch traced here: 89.4 us
  waiting for transfers between devices  23.1 us (26%)
  local copies, waits for them, and re-layouts  22.2 us (25%)
  matrix products  18.1 us (20%)
  starting transfers between devices  14.5 us (16%)
  other arithmetic  8.73 us (10%)
  between operations  2.8 us (3%)
    conv_general_dilated x2, matrix products, convolve(): lax.conv_general_dilated(field[None], kernel, (1, 1, 1), ((0, 0), (0, 0),...  18.1 us
    ppermute x2, waiting for transfers between devices, passed_along(): return lax.ppermute(block, axis, route)  16.3 us
    ppermute x2, starting transfers between devices, passed_along(): return lax.ppermute(block, axis, route)  5.89 us
    unnamed x23, local copies, waits for them, and re-layouts  5.65 us
    ppermute x2, waiting for transfers between devices, padded(): lax.ppermute(lax.slice_in_dim(block, block.shape[dim] - width, None, axis...  5.01 us
    ppermute x2, starting transfers between devices, padded(): lax.ppermute(lax.slice_in_dim(block, block.shape[dim] - width, None, axis...  4.77 us
    ppermute x2, starting transfers between devices, padded(): lax.ppermute(lax.slice_in_dim(block, 0, width, axis=dim), axis, backward)  3.86 us
    select_n x2, other arithmetic, attach(): return jnp.where((row_ids == place)[None, :, None, None], below, extended)  3.78 us
  transfers between devices with their start and end apart: 6, of which 5 were waited for; matrix products, arithmetic and copies ran while one was open for 8% of the time, Pallas kernels for 0%

commit v1 on v0

v1 whole, which is shorter than its diff:
```python
import functools

import jax
import jax.numpy as jnp
from jax import lax
from jax.experimental import pallas as pl
from jax.experimental.pallas import tpu as pltpu
from jax.sharding import PartitionSpec as P

F32 = jnp.float32
BF16 = jnp.bfloat16
AXES = ("tm", "tile")
FIRST_STEP = 2
SECOND_STEP = 4


def rotated(block, axis):
    count = lax.axis_size(axis)
    return lax.ppermute(block, axis, [(i, (i + 1) % count) for i in range(count)])


def routes(groups, tiles, step, side):
    pairs = []
    for g in range(groups):
        for t in range(tiles):
            if side == "chip":
                to = t ^ 1
            else:
                to = t + 1 if t % 2 else t - 1
            if 0 <= to < tiles:
                pairs.append((g * tiles + t, ((g + step) % groups) * tiles + to))
            elif step:
                pairs.append((g * tiles + t, ((g + step) % groups) * tiles + t))
            else:
                pairs.append((g * tiles + t, (g ^ 1) * tiles + t))
    return pairs


def down(v):
    n = v.shape[-2]
    ids = lax.broadcasted_iota(jnp.int32, v.shape, v.ndim - 2)
    return jnp.where(ids == 0, 0.0, pltpu.roll(v, 1, v.ndim - 2))


def up(v):
    n = v.shape[-2]
    ids = lax.broadcasted_iota(jnp.int32, v.shape, v.ndim - 2)
    return jnp.where(ids == n - 1, 0.0, pltpu.roll(v, n - 1, v.ndim - 2))


def fold_kernel(k1_hbm, w1_ref, k1_ref, sem):
    chunk = 32
    cin = k1_ref.shape[3]
    copies = [pltpu.make_async_copy(k1_hbm.at[a], k1_ref.at[a], sem.at[a]) for a in range(3)]
    for copy in copies:
        copy.start()

    def pairs(x, y, z):
        return (x, y + z), (x + y, z)

    for a in range(3):
        copies[a].wait()

        def part(s, _):
            r0 = pl.multiple_of(s * chunk, chunk)
            rows = pl.ds(r0, chunk)
            g = [[k1_ref[a, p, q, rows, :].astype(F32) for q in range(3)] for p in range(3)]
            by_row = [pairs(g[0][q], g[1][q], g[2][q]) for q in range(3)]
            for r in range(2):
                for i in range(2):
                    taps = pairs(by_row[0][r][i], by_row[1][r][i], by_row[2][r][i])
                    for c in range(2):
                        for j in range(2):
                            w1_ref[r, c, a, i, j, rows, :] = taps[c][j].astype(BF16)
            return 0

        lax.fori_loop(0, cin // chunk, part, 0)


def main_kernel(
    rows_ref, b1_ref, b2_ref, x_ref, prev_ref, cross_ref, chip_ref, dcross_ref, dchip_ref,
    w1_ref, w2_ref, out_ref, xs, hs, mix
):
    frames, cap, cols, ch = x_ref.shape
    tiles = lax.axis_size("tile")
    group = lax.axis_index("tm")
    tile = lax.axis_index("tile")
    length = rows_ref[tile]
    odd = lax.rem(tile, 2) == 1
    half = cap + 1
    hid = frames + 2
    mid = slice(ch, 2 * ch)

    zero = jnp.zeros((frames, cols, ch), BF16)
    has_cross = jnp.logical_and(tile > 0, tile < tiles - 1)
    for base, own, cr, ci in ((frames, x_ref, cross_ref, chip_ref), (0, prev_ref, dcross_ref, dchip_ref)):
        cross = jnp.where(has_cross, cr[:, 0], zero)
        chip = ci[:, 0]
        xs[base:base + frames, 1:cap + 1, :, mid] = own[...]
        xs[base:base + frames, 0, :, mid] = jnp.where(odd, chip, cross)
        xs[base:base + frames, cap + 1, :, mid] = zero
        xs[base:base + frames, length + 1, :, mid] = jnp.where(odd, cross, chip)

    def neighbours(f, _):
        z = xs[f, :, :, mid].astype(F32)
        xs[f, :, :, 0:ch] = down(z).astype(BF16)
        xs[f, :, :, 2 * ch:3 * ch] = up(z).astype(BF16)
        return 0

    lax.fori_loop(0, 2 * frames, neighbours, 0)

    @pl.when(group == 0)
    def _():
        first = xs[frames]
        for f in range(frames):
            xs[f] = first

    bias_one = b1_ref[...]
    top = tile == 0
    bottom = tile == tiles - 1

    def dot(lhs, rhs):
        return jnp.dot(lhs, rhs, preferred_element_type=F32)

    def first_conv(f, n):
        for phase in range(2):
            act = []
            for c in range(2):
                lhs = jnp.concatenate(
                    [
                        xs[pl.ds(f + a, n), i:i + half, :, c * ch:(c + 2) * ch].reshape(n * half * cols, 2 * ch)
                        for a in range(3) for i in range(2)
                    ],
                    axis=1,
                )
                v = dot(lhs, w1_ref[phase, c].reshape(12 * ch, ch)) + bias_one
                v = v / (1.0 + jnp.exp(-v))
                act.append(v.reshape(n, half, cols, ch))
            he, ho = act
            k = lax.broadcasted_iota(jnp.int32, he.shape, 1)
            if phase == 0:
                keep = jnp.logical_not(jnp.logical_and(bottom, k == length))
            else:
                keep = jnp.logical_not(jnp.logical_and(top, k == 0))
            he = jnp.where(keep, he, 0.0)
            ho = jnp.where(keep, ho, 0.0)
            for c, value in enumerate((down(ho), he, ho, up(he))):
                hs[phase, pl.ds(f, n), :, :, c * ch:(c + 1) * ch] = value.astype(BF16)

    for f in range(0, hid, FIRST_STEP):
        first_conv(f, FIRST_STEP)

    bias_two = b2_ref[...]

    def second_conv(f, n):
        for r in range(2):
            rows = ((1, 0), (0, 0), (1, 1)) if r == 0 else ((0, 0), (1, 1), (0, 1))
            sums = []
            for c in range(2):
                lhs = jnp.concatenate(
                    [
                        hs[phase, pl.ds(f + a, n), k:k + cap, :, c * ch:(c + 3) * ch].reshape(n * cap * cols, 3 * ch)
                        for a in range(3) for phase, k in rows
                    ],
                    axis=1,
                )
                v = dot(lhs, w2_ref[...].reshape(27 * ch, ch)) + bias_two
                sums.append(v.reshape(n, cap, cols, ch))
            for g in range(n):
                for i in range(cap):
                    residual = xs[frames + f + g, i + 1, :, mid].astype(F32)
                    keep = i < length
                    for c in range(2):
                        value = jnp.where(keep, sums[c][g, i] + residual, 0.0)
                        for part in range(ch // 128):
                            mix[r, g, i, part, pl.ds(c, cols, stride=2), :] = value[:, 128 * part:128 * (part + 1)]
                    for part in range(ch // 128):
                        lanes = slice(128 * part, 128 * (part + 1))
                        out_ref[f + g, 2 * i + r, :, lanes] = mix[r, g, i, part].astype(BF16)

    for f in range(0, frames, SECOND_STEP):
        second_conv(f, SECOND_STEP)


def local(latent, tile_rows, kernel_one, bias_one, kernel_two, bias_two):
    frames, cap, cols, ch = latent.shape
    groups, tiles = lax.axis_size("tm"), lax.axis_size("tile")
    tile = lax.axis_index("tile")
    last = lax.dynamic_slice_in_dim(tile_rows, tile, 1)[0] - 1
    odd = lax.rem(tile, 2) == 1
    to_cross = lax.dynamic_slice_in_dim(latent, jnp.where(odd, last, 0), 1, axis=1)
    to_chip = lax.dynamic_slice_in_dim(latent, jnp.where(odd, 0, last), 1, axis=1)
    prev = rotated(latent, "tm")
    cross = lax.ppermute(to_cross, AXES, routes(groups, tiles, 0, "cross"))
    dcross = lax.ppermute(to_cross, AXES, routes(groups, tiles, 1, "cross"))
    dchip = lax.ppermute(to_chip, AXES, routes(groups, tiles, 1, "chip"))
    chip = lax.ppermute(to_chip, AXES, routes(groups, tiles, 0, "chip"))

    vmem = pl.BlockSpec(memory_space=pltpu.VMEM)
    smem = pl.BlockSpec(memory_space=pltpu.SMEM)
    w1 = pl.pallas_call(
        fold_kernel,
        out_shape=pltpu.VMEM((2, 2, 3, 2, 2, ch, ch), BF16),
        in_specs=[pl.BlockSpec(memory_space=pl.ANY)],
        out_specs=vmem,
        scratch_shapes=[pltpu.VMEM(kernel_one.shape, BF16), pltpu.SemaphoreType.DMA((3,))],
        compiler_params=pltpu.CompilerParams(vmem_limit_bytes=16 << 20),
        cost_estimate=pl.CostEstimate(flops=0, bytes_accessed=10 << 20, transcendentals=0),
        name="fold",
    )(kernel_one)
    w1 = pltpu.with_memory_space_constraint(w1, pltpu.VMEM)
    w2 = pltpu.with_memory_space_constraint(kernel_two, pltpu.VMEM)

    hid, ext = frames + 2, cap + 2
    return pl.pallas_call(
        main_kernel,
        out_shape=jax.ShapeDtypeStruct((frames, 2 * cap, 2 * cols, ch), BF16),
        in_specs=[smem] + [vmem] * 10,
        out_specs=vmem,
        scratch_shapes=[
            pltpu.VMEM((2 * frames, ext, cols, 3 * ch), BF16),
            pltpu.VMEM((2, hid, cap + 1, cols, 4 * ch), BF16),
            pltpu.VMEM((2, SECOND_STEP, cap, ch // 128, 2 * cols, 128), F32),
        ],
        compiler_params=pltpu.CompilerParams(vmem_limit_bytes=36 << 20),
        cost_estimate=pl.CostEstimate(flops=13 << 30, bytes_accessed=2 << 20, transcendentals=0),
        name="decode",
    )(tile_rows, bias_one.reshape(1, ch), bias_two.reshape(1, ch), latent, prev, cross, chip, dcross, dchip, w1, w2)


def solution(mesh):
    in_specs = (P("tm", "tile", None, None), P(), P(), P(), P(), P())
    out_specs = P("tm", "tile", None, None)
    return jax.shard_map(local, mesh=mesh, in_specs=in_specs, out_specs=out_specs, check_vma=False)
```

time: 89.9 us -> 30.3 us (0.34)
  the two profiles are of different devices: /device:TPU:12 before, /device:TPU:0 now
where the time goes in v1:
time: 30.3 us; the launch traced here: 30.1 us
  Pallas kernels  17.6 us (58%)
  starting transfers between devices  6.14 us (20%)
  local copies, waits for them, and re-layouts  4.19 us (14%)
  waiting for transfers between devices  1.41 us (5%)
  between operations  0.73 us (2%)
    pallas_call x1, Pallas kernels, local(): pl.pallas_call(main_kernel, out_shape=jax.ShapeDtypeStruct((frames, 2 * c...  15.8 us
    ppermute x1, starting transfers between devices, rotated(): lax.ppermute(block, axis, [(i, (i + 1) % count) for i in range(count)])  2.94 us
    unnamed x12, local copies, waits for them, and re-layouts  2.02 us
    pallas_call x1, Pallas kernels, local(): pl.pallas_call(fold_kernel, out_shape=pltpu.VMEM((2, 2, 3, 2, 2, ch, ch),...  1.74 us
    ppermute x1, starting transfers between devices, local(): dcross = lax.ppermute(to_cross, AXES, routes(groups, tiles, 1, 'cross'))  1.49 us
    dynamic_slice x1, local copies, waits for them, and re-layouts, local(): last = lax.dynamic_slice_in_dim(tile_rows, tile, 1)[0] - 1  1.24 us
    ppermute x1, starting transfers between devices, local(): chip = lax.ppermute(to_chip, AXES, routes(groups, tiles, 0, 'chip'))  1 us
    dynamic_slice x1, local copies, waits for them, and re-layouts, local(): lax.dynamic_slice_in_dim(latent, jnp.where(odd, 0, last), 1, axis=1)  0.93 us
  transfers between devices with their start and end apart: 5, of which 2 were waited for; matrix products, arithmetic and copies ran while one was open for 7% of the time, Pallas kernels for 6%

profile of v1, /device:TPU:0, one launch (start us, length us, event | category | flops | bytes accessed | tf_op | source)
XLA Modules:
  0.0 30.1 jit_solution(18317485957775529847)
XLA Ops:
  0.0 2.9 %collective-permute-start = (bf16[4,4,32,256]{3,2,1,0:T(8,128)(2,1)}, bf16[4,4,32,256]{3,2,1,0:T(8,128)(2,1)S(1)}, u32[]{:S(2)}, u32[]{:S(2)}) collective-permute-start(bf16[4,4,32,256]{3,2,1,0:T(8,128)(2,1)} %x_ref.1), channel_id=1, source_target_pairs={{0,8},{8,16},{16,24},{24,0},{1,9},{9,17},{17,25},{25,1},{2,10},{10... | collective-permute-start | bytes 786440 | tf_op jit(solution)/shard_map/ppermute | solution.py:19
  2.9 1.2 %dynamic_slice.9 = s32[1]{0:T(128)} dynamic-slice(s32[8]{0:T(128)} %rows_ref.1, s32[]{:T(128)S(6)} %select_n.17), dynamic_slice_sizes={1} | dynamic-slice | bytes 12 | tf_op jit(solution)/shard_map/dynamic_slice | solution.py:189
  4.8 0.9 %constant_dynamic-slice_fusion = (bf16[4,1,32,256]{3,2,1,0:T(8,128)(2,1)S(1)}, bf16[4,1,32,256]{3,2,1,0:T(8,128)(2,1)S(1)}) fusion(bf16[4,4,32,256]{3,2,1,0:T(8,128)(2,1)} %x_ref.1, s32[]{:T(128)S(6)} %select_n.21, s32[]{:T(128)S(6)} %select_n.19), kind=kLoop, calls=%fused_computation | loop fusion | bytes 262152 | tf_op jit(solution)/shard_map/dynamic_slice | solution.py:192
  5.8 0.7 %collective-permute-start.4 = (bf16[4,1,32,256]{3,2,1,0:T(8,128)(2,1)S(1)}, bf16[4,1,32,256]{3,2,1,0:T(8,128)(2,1)S(1)}, u32[]{:S(2)}, u32[]{:S(2)}) collective-permute-start(bf16[4,1,32,256]{3,2,1,0:T(8,128)(2,1)S(1)} %get-tuple-element.5), channel_id=1, source_target_pairs={{0,9},{1,8},{2,11},{3,10},{4,13},{5,12},{6,15},{7,14},{8,17},{9,16... | collective-permute-start | bytes 196616 | tf_op jit(solution)/shard_map/ppermute | solution.py:196
  6.4 1.0 %collective-permute-start.2 = (bf16[4,1,32,256]{3,2,1,0:T(8,128)(2,1)S(1)}, bf16[4,1,32,256]{3,2,1,0:T(8,128)(2,1)S(1)}, u32[]{:S(2)}, u32[]{:S(2)}) collective-permute-start(bf16[4,1,32,256]{3,2,1,0:T(8,128)(2,1)S(1)} %get-tuple-element.5), channel_id=1, source_target_pairs={{0,1},{1,0},{2,3},{3,2},{4,5},{5,4},{6,7},{7,6},{8,9},{9,8},{10,11... | collective-permute-start | bytes 196616 | tf_op jit(solution)/shard_map/ppermute | solution.py:197
  7.4 0.0 copy-start.3
  7.4 0.0 copy-start.5
  7.4 1.5 %collective-permute-start.3 = (bf16[4,1,32,256]{3,2,1,0:T(8,128)(2,1)S(1)}, bf16[4,1,32,256]{3,2,1,0:T(8,128)(2,1)S(1)}, u32[]{:S(2)}, u32[]{:S(2)}) collective-permute-start(bf16[4,1,32,256]{3,2,1,0:T(8,128)(2,1)S(1)} %get-tuple-element.6), channel_id=1, source_target_pairs={{0,8},{1,10},{2,9},{3,12},{4,11},{5,14},{6,13},{7,15},{8,16},{9,18... | collective-permute-start | bytes 196616 | tf_op jit(solution)/shard_map/ppermute | solution.py:195
  8.9 0.0 collective-permute-start.1
  9.0 2.0 %copy-done = bf16[3,3,3,256,256]{4,3,2,1,0:T(8,128)(2,1)S(1)} copy-done((bf16[3,3,3,256,256]{4,3,2,1,0:T(8,128)(2,1)S(1)}, bf16[3,3,3,256,256]{4,3,2,1,0:T(8,128)(2,1)}, u32[]{:S(2)}) %copy-start) | copy-done | bytes 3538968
  11.0 0.0 copy-start.1
  11.0 0.0 copy-start.2
  11.0 1.7 %fold.1.w1_ref = bf16[2,2,3,2,2,256,256]{6,5,4,3,2,1,0:T(8,128)(2,1)S(1)} custom-call(bf16[3,3,3,256,256]{4,3,2,1,0:T(8,128)(2,1)S(1)} %copy-done), custom_call_target="tpu_custom_call" | custom-call | bytes 10485760 | tf_op jit(solution)/shard_map/fold/pallas_call | solution.py:201
  12.7 0.0 collective-permute-done.4.dchip_ref
  12.8 0.0 collective-permute-done.2.chip_ref
  12.8 0.5 %collective-permute-done.3.dcross_ref = bf16[4,1,32,256]{3,2,1,0:T(8,128)(2,1)S(1)} collective-permute-done((bf16[4,1,32,256]{3,2,1,0:T(8,128)(2,1)S(1)}, bf16[4,1,32,256]{3,2,1,0:T(8,128)(2,1)S(1)}, u32[]{:S(2)}, u32[]{:S(2)}) %collective-permute-start.3) | collective-permute-done | bytes 65568 | tf_op jit(solution)/shard_map/ppermute | solution.py:195
  13.3 0.9 %collective-permute-done.1.cross_ref = bf16[4,1,32,256]{3,2,1,0:T(8,128)(2,1)S(1)} collective-permute-done((bf16[4,1,32,256]{3,2,1,0:T(8,128)(2,1)S(1)}, bf16[4,1,32,256]{3,2,1,0:T(8,128)(2,1)S(1)}, u32[]{:S(2)}, u32[]{:S(2)}) %collective-permute-start.1) | collective-permute-done | bytes 65568 | tf_op jit(solution)/shard_map/ppermute | solution.py:194
  14.2 0.0 collective-permute-done.prev_ref
  14.2 0.0 copy-done.3
  14.2 0.0 copy-done.5
  14.2 0.0 copy-done.1
  14.2 0.0 copy-done.2
  14.2 0.0 copy-done.4
  14.2 15.8 %decode.1 = bf16[4,8,64,256]{3,2,1,0:T(8,128)(2,1)} custom-call(s32[8]{0:T(128)S(1)} %copy-done.5, f32[1,256]{1,0:T(1,128)S(1)} %bitcast.3, f32[1,256]{1,0:T(1,128)S(1)} %bitcast.4, bf16[4,4,32,256]{3,2,1,0:T(8,128)(2,1)S(1)} %copy-done.1, bf16[4,4,32,256]{3,2,1,0:T(8,128)(2,1)S(1)} %collective-permute-done.prev_ref, ...), custom_call_target="tpu_custom_call" | custom-call | flops 13958643712 | bytes 2097152 | tf_op jit(solution)/shard_map/decode/pallas_call | solution.py:215
  (2 shorter events, 0.0 us)
Async XLA Ops:
  0.0 14.2 %collective-permute-start = (bf16[4,4,32,256]{3,2,1,0:T(8,128)(2,1)}, bf16[4,4,32,256]{3,2,1,0:T(8,128)(2,1)S(1)}, u32[]{:S(2)}, u32[]{:S(2)}) collective-permute-start(bf16[4,4,32,256]{3,2,1,0:T(8,128)(2,1)} %x_ref.1), channel_id=1, source_target_pairs={{0,8},{8,16},{16,24},{24,0},{1,9},{9,17},{17,25},{25,1},{2,10},{10... | collective-permute-start | bytes 786440 | tf_op jit(solution)/shard_map/ppermute | solution.py:19
  5.8 7.0 %collective-permute-start.4 = (bf16[4,1,32,256]{3,2,1,0:T(8,128)(2,1)S(1)}, bf16[4,1,32,256]{3,2,1,0:T(8,128)(2,1)S(1)}, u32[]{:S(2)}, u32[]{:S(2)}) collective-permute-start(bf16[4,1,32,256]{3,2,1,0:T(8,128)(2,1)S(1)} %get-tuple-element.5), channel_id=1, source_target_pairs={{0,9},{1,8},{2,11},{3,10},{4,13},{5,12},{6,15},{7,14},{8,17},{9,16... | collective-permute-start | bytes 196616 | tf_op jit(solution)/shard_map/ppermute | solution.py:196
  6.4 6.3 %collective-permute-start.2 = (bf16[4,1,32,256]{3,2,1,0:T(8,128)(2,1)S(1)}, bf16[4,1,32,256]{3,2,1,0:T(8,128)(2,1)S(1)}, u32[]{:S(2)}, u32[]{:S(2)}) collective-permute-start(bf16[4,1,32,256]{3,2,1,0:T(8,128)(2,1)S(1)} %get-tuple-element.5), channel_id=1, source_target_pairs={{0,1},{1,0},{2,3},{3,2},{4,5},{5,4},{6,7},{7,6},{8,9},{9,8},{10,11... | collective-permute-start | bytes 196616 | tf_op jit(solution)/shard_map/ppermute | solution.py:197
  7.4 6.7 %copy-start.3 = (f32[256]{0:T(256)S(1)}, f32[256]{0:T(256)}, u32[]{:S(2)}) copy-start(f32[256]{0:T(256)} %param.9) | copy-start | bytes 3076
  7.4 6.7 %copy-start.5 = (s32[8]{0:T(128)S(1)}, s32[8]{0:T(128)}, u32[]{:S(2)}) copy-start(s32[8]{0:T(128)} %rows_ref.1) | copy-start | bytes 100
  7.4 5.9 %collective-permute-start.3 = (bf16[4,1,32,256]{3,2,1,0:T(8,128)(2,1)S(1)}, bf16[4,1,32,256]{3,2,1,0:T(8,128)(2,1)S(1)}, u32[]{:S(2)}, u32[]{:S(2)}) collective-permute-start(bf16[4,1,32,256]{3,2,1,0:T(8,128)(2,1)S(1)} %get-tuple-element.6), channel_id=1, source_target_pairs={{0,8},{1,10},{2,9},{3,12},{4,11},{5,14},{6,13},{7,15},{8,16},{9,18... | collective-permute-start | bytes 196616 | tf_op jit(solution)/shard_map/ppermute | solution.py:195
  8.9 5.2 %collective-permute-start.1 = (bf16[4,1,32,256]{3,2,1,0:T(8,128)(2,1)S(1)}, bf16[4,1,32,256]{3,2,1,0:T(8,128)(2,1)S(1)}, u32[]{:S(2)}, u32[]{:S(2)}) collective-permute-start(bf16[4,1,32,256]{3,2,1,0:T(8,128)(2,1)S(1)} %get-tuple-element.6), channel_id=1, source_target_pairs={{0,8},{1,2},{2,1},{3,4},{4,3},{5,6},{6,5},{7,15},{8,0},{9,10},{10,... | collective-permute-start | bytes 196616 | tf_op jit(solution)/shard_map/ppermute | solution.py:194
  9.0 2.0 %copy-start = (bf16[3,3,3,256,256]{4,3,2,1,0:T(8,128)(2,1)S(1)}, bf16[3,3,3,256,256]{4,3,2,1,0:T(8,128)(2,1)}, u32[]{:S(2)}) copy-start(bf16[3,3,3,256,256]{4,3,2,1,0:T(8,128)(2,1)} %k1_hbm.1) | copy-start | bytes 10616836
  11.0 3.2 %copy-start.1 = (bf16[4,4,32,256]{3,2,1,0:T(8,128)(2,1)S(1)}, bf16[4,4,32,256]{3,2,1,0:T(8,128)(2,1)}, u32[]{:S(2)}) copy-start(bf16[4,4,32,256]{3,2,1,0:T(8,128)(2,1)} %x_ref.1) | copy-start | bytes 786436
  11.0 3.2 %copy-start.2 = (bf16[3,3,3,256,256]{4,3,2,1,0:T(8,128)(2,1)S(1)}, bf16[3,3,3,256,256]{4,3,2,1,0:T(8,128)(2,1)}, u32[]{:S(2)}) copy-start(bf16[3,3,3,256,256]{4,3,2,1,0:T(8,128)(2,1)} %w2_ref.1) | copy-start | bytes 10616836
  11.0 3.2 %copy-start.4 = (f32[256]{0:T(256)S(1)}, f32[256]{0:T(256)}, u32[]{:S(2)}) copy-start(f32[256]{0:T(256)} %param.11) | copy-start | bytes 3076

commit v2 on v1

v2 whole, which is shorter than its diff:
```python
import functools

import jax
import jax.numpy as jnp
from jax import lax
from jax.experimental import pallas as pl
from jax.experimental.pallas import tpu as pltpu
from jax.sharding import PartitionSpec as P

F32 = jnp.float32
BF16 = jnp.bfloat16
AXES = ("tm", "tile")
FIRST_STEP = 2


def rotated(block, axis):
    count = lax.axis_size(axis)
    return lax.ppermute(block, axis, [(i, (i + 1) % count) for i in range(count)])


def routes(groups, tiles, step, side):
    pairs = []
    for g in range(groups):
        for t in range(tiles):
            if side == "chip":
                to = t ^ 1
            else:
                to = t + 1 if t % 2 else t - 1
            if 0 <= to < tiles:
                pairs.append((g * tiles + t, ((g + step) % groups) * tiles + to))
            elif step:
                pairs.append((g * tiles + t, ((g + step) % groups) * tiles + t))
            else:
                pairs.append((g * tiles + t, g * tiles + tiles - 1 - t))
    return pairs


def down(v):
    n = v.shape[-2]
    ids = lax.broadcasted_iota(jnp.int32, v.shape, v.ndim - 2)
    return jnp.where(ids == 0, 0.0, pltpu.roll(v, 1, v.ndim - 2))


def up(v):
    n = v.shape[-2]
    ids = lax.broadcasted_iota(jnp.int32, v.shape, v.ndim - 2)
    return jnp.where(ids == n - 1, 0.0, pltpu.roll(v, n - 1, v.ndim - 2))


def pick_kernel(rows_hbm, x_hbm, cross_ref, chip_ref, rows_ref, x_ref, sem):
    copies = [
        pltpu.make_async_copy(rows_hbm, rows_ref, sem.at[0]),
        pltpu.make_async_copy(x_hbm, x_ref, sem.at[1]),
    ]
    for copy in copies:
        copy.start()
    for copy in copies:
        copy.wait()
    tile = lax.axis_index("tile")
    last = rows_ref[tile] - 1
    odd = lax.rem(tile, 2) == 1
    cross_ref[:, 0] = x_ref[:, jnp.where(odd, last, 0)]
    chip_ref[:, 0] = x_ref[:, jnp.where(odd, 0, last)]


def assemble(xs, own, cross_ref, chip_ref, chip_row, length):
    frames, cap, cols, ch = own.shape
    tile = lax.axis_index("tile")
    odd = lax.rem(tile, 2) == 1
    mid = slice(ch, 2 * ch)
    zero = jnp.zeros((frames, cols, ch), BF16)
    has_cross = jnp.logical_and(tile > 0, tile < lax.axis_size("tile") - 1)
    cross = jnp.where(has_cross, cross_ref[:, 0], zero)
    chip = chip_ref[:, chip_row]
    xs[:, 1:cap + 1, :, mid] = own[...]
    xs[:, 0, :, mid] = jnp.where(odd, chip, cross)
    xs[:, cap + 1, :, mid] = zero
    xs[:, length + 1, :, mid] = jnp.where(odd, cross, chip)

    def neighbours(f, _):
        z = xs[f, :, :, mid].astype(F32)
        xs[f, :, :, 0:ch] = down(z).astype(BF16)
        xs[f, :, :, 2 * ch:3 * ch] = up(z).astype(BF16)
        return 0

    lax.fori_loop(0, frames, neighbours, 0)


def dot(lhs, rhs):
    return jnp.dot(lhs, rhs, preferred_element_type=F32)


def first_conv(sources, w1_ref, bias, hs, f, length):
    n = len(sources)
    _, _, half, cols, wide = hs.shape
    ch = wide // 4
    tile = lax.axis_index("tile")
    top = tile == 0
    bottom = tile == lax.axis_size("tile") - 1
    for phase in range(2):
        act = []
        for c in range(2):
            lhs = jnp.concatenate(
                [
                    jnp.concatenate(
                        [
                            ref[g, i:i + half, :, c * ch:(c + 2) * ch].reshape(half * cols, 2 * ch)
                            for a in range(3) for i in range(2) for ref, g in [taps[a]]
                        ],
                        axis=1,
                    )
                    for taps in sources
                ],
                axis=0,
            )
            v = dot(lhs, w1_ref[phase, c].reshape(12 * ch, ch)) + bias
            v = v / (1.0 + jnp.exp(-v))
            act.append(v.reshape(n, half, cols, ch))
        he, ho = act
        k = lax.broadcasted_iota(jnp.int32, he.shape, 1)
        if phase == 0:
            keep = jnp.logical_not(jnp.logical_and(bottom, k == length))
        else:
            keep = jnp.logical_not(jnp.logical_and(top, k == 0))
        he = jnp.where(keep, he, 0.0)
        ho = jnp.where(keep, ho, 0.0)
        for c, value in enumerate((down(ho) - ho, he + ho, ho - he, he - up(he))):
            hs[phase, f:f + n, :, :, c * ch:(c + 1) * ch] = value.astype(BF16)


def fold_kernel(k1_hbm, k2_hbm, w1_ref, w2_ref, k1_ref, k2_ref, sem):
    chunk = 32
    cin = k1_ref.shape[3]
    copies = [
        pltpu.make_async_copy(source.at[a], target.at[a], sem.at[3 * n + a])
        for n, (source, target) in enumerate(((k1_hbm, k1_ref), (k2_hbm, k2_ref))) for a in range(3)
    ]
    for copy in copies:
        copy.start()

    def pairs(x, y, z):
        return (x, y + z), (x + y, z)

    for a in range(3):
        copies[a].wait()

        def part(s, _):
            r0 = pl.multiple_of(s * chunk, chunk)
            rows = pl.ds(r0, chunk)
            g = [[k1_ref[a, p, q, rows, :].astype(F32) for q in range(3)] for p in range(3)]
            by_row = [pairs(g[0][q], g[1][q], g[2][q]) for q in range(3)]
            for r in range(2):
                for i in range(2):
                    taps = pairs(by_row[0][r][i], by_row[1][r][i], by_row[2][r][i])
                    for c in range(2):
                        for j in range(2):
                            w1_ref[r, c, a, i, j, rows, :] = taps[c][j].astype(BF16)
            return 0

        lax.fori_loop(0, cin // chunk, part, 0)

    for a in range(3):
        copies[3 + a].wait()

        def spread(s, _):
            r0 = pl.multiple_of(s * chunk, chunk)
            rows = pl.ds(r0, chunk)
            for p in range(3):
                x, y, z = (k2_ref[a, p, q, rows, :] for q in range(3))
                even = (x.astype(F32) + z.astype(F32)) * 0.5
                odd = y.astype(F32) * 0.5
                w2_ref[0, a, p, rows, :] = x
                w2_ref[1, a, p, rows, :] = (even + odd).astype(BF16)
                w2_ref[2, a, p, rows, :] = (even - odd).astype(BF16)
                w2_ref[3, a, p, rows, :] = z
            return 0

        lax.fori_loop(0, cin // chunk, spread, 0)


def own_kernel(rows_ref, b1_ref, x_ref, cross_ref, chip_ref, w1_ref, xs, hs):
    frames = x_ref.shape[0]
    length = rows_ref[lax.axis_index("tile")]
    assemble(xs, x_ref, cross_ref, chip_ref, 0, length)
    own = hs.shape[1]
    sources = [[(xs, frames - 2 - own + n + a) for a in range(3)] for n in range(own)]
    first_conv(sources, w1_ref, b1_ref[...], hs, 0, length)


def rest_kernel(
    rows_ref, b1_ref, b2_ref, prev_ref, dcross_ref, dchip_ref, xo, ho, w1_ref, w2_ref, out_ref, xp, hp, mix
):
    frames, cap, cols, ch = prev_ref.shape
    tile = lax.axis_index("tile")
    length = rows_ref[tile]
    assemble(xp, prev_ref, dcross_ref, dchip_ref, 0, length)

    @pl.when(lax.axis_index("tm") == 0)
    def _():
        first = xo[0]
        for f in range(frames):
            xp[f] = first

    shared = hp.shape[1]
    source = [(xp, f) for f in range(frames)] + [(xo, f) for f in range(frames)]
    for f in range(0, shared, FIRST_STEP):
        first_conv(
            [[source[f + n + a] for a in range(3)] for n in range(FIRST_STEP)], w1_ref, b1_ref[...], hp, f, length
        )

    bias_two = b2_ref[...]
    hidden = [(hp, f) for f in range(shared)] + [(ho, f) for f in range(ho.shape[1])]
    for r in range(2):
        rows = ((1, 0), (0, 0), (1, 1)) if r == 0 else ((0, 0), (1, 1), (0, 1))
        m = []
        for c in range(4):
            lhs = jnp.concatenate(
                [
                    jnp.concatenate(
                        [
                            ref[phase, g, k:k + cap, :, c * ch:(c + 1) * ch].reshape(cap * cols, ch)
                            for a in range(3) for phase, k in rows for ref, g in [hidden[f + a]]
                        ],
                        axis=1,
                    )
                    for f in range(frames)
                ],
                axis=0,
            )
            m.append(dot(lhs, w2_ref[c].reshape(9 * ch, ch)))
        sums = [
            (v + bias_two).reshape(frames, cap, cols, ch) for v in (m[0] + (m[1] + m[2]), (m[1] - m[2]) - m[3])
        ]
        for f in range(frames):
            for i in range(cap):
                residual = xo[f, i + 1, :, ch:2 * ch].astype(F32)
                keep = i < length
                for c in range(2):
                    value = jnp.where(keep, sums[c][f, i] + residual, 0.0)
                    for part in range(ch // 128):
                        mix[r, f, i, part, pl.ds(c, cols, stride=2), :] = value[:, 128 * part:128 * (part + 1)]
                for part in range(ch // 128):
                    lanes = slice(128 * part, 128 * (part + 1))
                    out_ref[f, 2 * i + r, :, lanes] = mix[r, f, i, part].astype(BF16)


def in_hbm(value):
    return pltpu.with_memory_space_constraint(value, pltpu.HBM)


def in_vmem(value):
    return pltpu.with_memory_space_constraint(value, pltpu.VMEM)


def local(latent, tile_rows, kernel_one, bias_one, kernel_two, bias_two):
    frames, cap, cols, ch = latent.shape
    groups, tiles = lax.axis_size("tm"), lax.axis_size("tile")
    vmem = pl.BlockSpec(memory_space=pltpu.VMEM)
    smem = pl.BlockSpec(memory_space=pltpu.SMEM)
    hbm = pl.BlockSpec(memory_space=pltpu.HBM)
    bias_one, bias_two = bias_one.reshape(1, ch), bias_two.reshape(1, ch)

    prev = rotated(latent, "tm")
    rim = pltpu.VMEM((frames, 1, cols, ch), BF16)
    to_cross, to_chip = pl.pallas_call(
        pick_kernel,
        out_shape=(rim, rim),
        in_specs=[hbm, hbm],
        out_specs=(vmem, vmem),
        scratch_shapes=[
            pltpu.SMEM(tile_rows.shape, jnp.int32),
            pltpu.VMEM(latent.shape, BF16),
            pltpu.SemaphoreType.DMA((2,)),
        ],
        compiler_params=pltpu.CompilerParams(vmem_limit_bytes=4 << 20),
        cost_estimate=pl.CostEstimate(flops=0, bytes_accessed=1 << 19, transcendentals=0),
        name="pick",
    )(in_hbm(tile_rows), in_hbm(latent))
    chip = lax.ppermute(to_chip, AXES, routes(groups, tiles, 0, "chip"))
    cross = lax.ppermute(to_cross, AXES, routes(groups, tiles, 0, "cross"))
    dcross = lax.ppermute(to_cross, AXES, routes(groups, tiles, 1, "cross"))
    dchip = lax.ppermute(to_chip, AXES, routes(groups, tiles, 1, "chip"))

    w1, w2 = pl.pallas_call(
        fold_kernel,
        out_shape=(pltpu.VMEM((2, 2, 3, 2, 2, ch, ch), BF16), pltpu.VMEM((4, 3, 3, ch, ch), BF16)),
        in_specs=[hbm, hbm],
        out_specs=(vmem, vmem),
        scratch_shapes=[
            pltpu.VMEM(kernel_one.shape, BF16),
            pltpu.VMEM(kernel_two.shape, BF16),
            pltpu.SemaphoreType.DMA((6,)),
        ],
        compiler_params=pltpu.CompilerParams(vmem_limit_bytes=16 << 20),
        cost_estimate=pl.CostEstimate(flops=0, bytes_accessed=8 << 20, transcendentals=0),
        name="fold",
    )(in_hbm(kernel_one), in_hbm(kernel_two))
    w1, w2 = in_vmem(w1), in_vmem(w2)

    own = frames - 2
    xo, ho = pl.pallas_call(
        own_kernel,
        out_shape=(
            pltpu.VMEM((frames, cap + 2, cols, 3 * ch), BF16),
            pltpu.VMEM((2, own, cap + 1, cols, 4 * ch), BF16),
        ),
        in_specs=[smem] + [vmem] * 5,
        out_specs=(vmem, vmem),
        compiler_params=pltpu.CompilerParams(vmem_limit_bytes=24 << 20),
        cost_estimate=pl.CostEstimate(flops=0, bytes_accessed=8 << 20, transcendentals=0),
        name="own",
    )(tile_rows, bias_one, latent, cross, chip, w1)

    return pl.pallas_call(
        rest_kernel,
        out_shape=jax.ShapeDtypeStruct((frames, 2 * cap, 2 * cols, ch), BF16),
        in_specs=[smem] + [vmem] * 9,
        out_specs=vmem,
        scratch_shapes=[
            pltpu.VMEM((frames, cap + 2, cols, 3 * ch), BF16),
            pltpu.VMEM((2, frames, cap + 1, cols, 4 * ch), BF16),
            pltpu.VMEM((2, frames, cap, ch // 128, 2 * cols, 128), F32),
        ],
        compiler_params=pltpu.CompilerParams(vmem_limit_bytes=36 << 20),
        cost_estimate=pl.CostEstimate(flops=10 << 30, bytes_accessed=2 << 20, transcendentals=0),
        name="rest",
    )(
        tile_rows, bias_one, bias_two, prev, dcross, dchip,
        in_vmem(xo), in_vmem(ho), w1, w2,
    )


def solution(mesh):
    in_specs = (P("tm", "tile", None, None), P(), P(), P(), P(), P())
    out_specs = P("tm", "tile", None, None)
    return jax.shard_map(local, mesh=mesh, in_specs=in_specs, out_specs=out_specs, check_vma=False)
```

time: 30.3 us -> 28.2 us (0.931)
  local copies, waits for them, and re-layouts: 4.19 us -> 0.02 us
  starting transfers between devices: 6.14 us -> 8.4 us
  Pallas kernels: 17.6 us -> 19.4 us
  waiting for transfers between devices: 1.41 us -> 0.01 us
  between operations: 0.73 us -> 0.11 us
    ppermute x1, starting transfers between devices: 0.05 us -> 2.83 us  [local(): cross = lax.ppermute(to_cross, AXES, routes(groups, tiles, 0, 'cross'))]
    dynamic_slice x2 -> x0, local copies, waits for them, and re-layouts: 2.17 us -> none  [the longest x1 1.24 us: local(): last = lax.dynamic_slice_in_dim(tile_rows, tile, 1)[0] - 1]
    unnamed x12 -> x8, local copies, waits for them, and re-layouts: 2.02 us -> 0.02 us
    pallas_call x2 -> x4, Pallas kernels: 17.6 us -> 19.4 us  [the longest x1 11.7 us: local(): pl.pallas_call(rest_kernel, out_shape=jax.ShapeDtypeStruct((frames, 2 * c...]
    ppermute x1, starting transfers between devices: 1 us -> 0.01 us  [local(): chip = lax.ppermute(to_chip, AXES, routes(groups, tiles, 0, 'chip'))]
    ppermute x1, waiting for transfers between devices: 0.86 us -> 0.01 us  [local(): cross = lax.ppermute(to_cross, AXES, routes(groups, tiles, 0, 'cross'))]
    ppermute x1, waiting for transfers between devices: 0.55 us -> 0.01 us  [local(): dcross = lax.ppermute(to_cross, AXES, routes(groups, tiles, 1, 'cross'))]
    ppermute x1, starting transfers between devices: 0.66 us -> 1.09 us  [local(): dchip = lax.ppermute(to_chip, AXES, routes(groups, tiles, 1, 'chip'))]
  transfers between devices with their start and end apart: 5 -> 5, of which waited for: 2 -> 0; matrix products, arithmetic and copies ran while one was open for 7% -> 0% of each run, Pallas kernels for 6% -> 28%
where the time goes in v2:
time: 28.2 us; the launch traced here: 28 us
  Pallas kernels  19.4 us (69%)
  starting transfers between devices  8.4 us (30%)
    pallas_call x1, Pallas kernels, local(): pl.pallas_call(rest_kernel, out_shape=jax.ShapeDtypeStruct((frames, 2 * c...  11.7 us
    pallas_call x1, Pallas kernels, local(): pl.pallas_call(own_kernel, out_shape=(pltpu.VMEM((frames, cap + 2, cols,...  3.37 us
    pallas_call x1, Pallas kernels, local(): pl.pallas_call(fold_kernel, out_shape=(pltpu.VMEM((2, 2, 3, 2, 2, ch, ch)...  3.34 us
    ppermute x1, starting transfers between devices, rotated(): lax.ppermute(block, axis, [(i, (i + 1) % count) for i in range(count)])  2.94 us
    ppermute x1, starting transfers between devices, local(): cross = lax.ppermute(to_cross, AXES, routes(groups, tiles, 0, 'cross'))  2.83 us
    ppermute x1, starting transfers between devices, local(): dcross = lax.ppermute(to_cross, AXES, routes(groups, tiles, 1, 'cross'))  1.54 us
    ppermute x1, starting transfers between devices, local(): dchip = lax.ppermute(to_chip, AXES, routes(groups, tiles, 1, 'chip'))  1.09 us
    pallas_call x1, Pallas kernels, local(): pl.pallas_call(pick_kernel, out_shape=(rim, rim), in_specs=[hbm, hbm], ou...  1.01 us
  transfers between devices with their start and end apart: 5, of which 0 were waited for; matrix products, arithmetic and copies ran while one was open for 0% of the time, Pallas kernels for 28%

profile of v2, /device:TPU:0, one launch (start us, length us, event | category | flops | bytes accessed | tf_op | source)
XLA Modules:
  0.0 28.0 jit_solution(1321244989852089440)
XLA Ops:
  0.0 2.9 %collective-permute-start = (bf16[4,4,32,256]{3,2,1,0:T(8,128)(2,1)}, bf16[4,4,32,256]{3,2,1,0:T(8,128)(2,1)S(1)}, u32[]{:S(2)}, u32[]{:S(2)}) collective-permute-start(bf16[4,4,32,256]{3,2,1,0:T(8,128)(2,1)} %x_ref.1), channel_id=1, source_target_pairs={{0,8},{8,16},{16,24},{24,0},{1,9},{9,17},{17,25},{25,1},{2,10},{10... | collective-permute-start | bytes 786440 | tf_op jit(solution)/shard_map/ppermute | solution.py:18
  2.9 1.0 %pick.1 = (bf16[4,1,32,256]{3,2,1,0:T(8,128)(2,1)S(1)}, bf16[4,1,32,256]{3,2,1,0:T(8,128)(2,1)S(1)}) custom-call(s32[8]{0:T(128)} %rows_ref.3, bf16[4,4,32,256]{3,2,1,0:T(8,128)(2,1)} %x_ref.1), custom_call_target="tpu_custom_call" | custom-call | bytes 524288 | tf_op jit(solution)/shard_map/pick/pallas_call | solution.py:265
  4.0 2.8 %collective-permute-start.3 = (bf16[4,1,32,256]{3,2,1,0:T(8,128)(2,1)S(1)}, bf16[4,1,32,256]{3,2,1,0:T(8,128)(2,1)S(1)}, u32[]{:S(2)}, u32[]{:S(2)}) collective-permute-start(bf16[4,1,32,256]{3,2,1,0:T(8,128)(2,1)S(1)} %get-tuple-element.11), channel_id=1, source_target_pairs={{0,7},{1,2},{2,1},{3,4},{4,3},{5,6},{6,5},{7,0},{8,15},{9,10},{10,... | collective-permute-start | bytes 196616 | tf_op jit(solution)/shard_map/ppermute | solution.py:280
  6.8 0.0 copy-start
  6.8 0.0 copy-start.1
  6.8 0.0 copy-start.2
  6.8 0.0 collective-permute-start.4
  6.8 1.5 %collective-permute-start.1 = (bf16[4,1,32,256]{3,2,1,0:T(8,128)(2,1)S(1)}, bf16[4,1,32,256]{3,2,1,0:T(8,128)(2,1)S(1)}, u32[]{:S(2)}, u32[]{:S(2)}) collective-permute-start(bf16[4,1,32,256]{3,2,1,0:T(8,128)(2,1)S(1)} %get-tuple-element.11), channel_id=1, source_target_pairs={{0,8},{1,10},{2,9},{3,12},{4,11},{5,14},{6,13},{7,15},{8,16},{9,18... | collective-permute-start | bytes 196616 | tf_op jit(solution)/shard_map/ppermute | solution.py:281
  8.3 1.1 %collective-permute-start.2 = (bf16[4,1,32,256]{3,2,1,0:T(8,128)(2,1)S(1)}, bf16[4,1,32,256]{3,2,1,0:T(8,128)(2,1)S(1)}, u32[]{:S(2)}, u32[]{:S(2)}) collective-permute-start(bf16[4,1,32,256]{3,2,1,0:T(8,128)(2,1)S(1)} %get-tuple-element.12), channel_id=1, source_target_pairs={{0,9},{1,8},{2,11},{3,10},{4,13},{5,12},{6,15},{7,14},{8,17},{9,16... | collective-permute-start | bytes 196616 | tf_op jit(solution)/shard_map/ppermute | solution.py:282
  9.4 3.3 %fold.1 = (bf16[2,2,3,2,2,256,256]{6,5,4,3,2,1,0:T(8,128)(2,1)S(1)}, bf16[4,3,3,256,256]{4,3,2,1,0:T(8,128)(2,1)S(1)}) custom-call(bf16[3,3,3,256,256]{4,3,2,1,0:T(8,128)(2,1)} %k1_hbm.1, bf16[3,3,3,256,256]{4,3,2,1,0:T(8,128)(2,1)} %k2_hbm.1), custom_call_target="tpu_custom_call" | custom-call | bytes 8388608 | tf_op jit(solution)/shard_map/fold/pallas_call | solution.py:284
  12.8 0.0 copy-start.3
  12.8 0.0 collective-permute-done.3.cross_ref
  12.8 0.0 collective-permute-done.4.chip_ref
  12.8 0.0 copy-done
  12.8 0.0 copy-done.1
  12.8 0.0 copy-done.2
  12.8 3.4 %own.1 = (bf16[4,6,32,768]{3,2,1,0:T(8,128)(2,1)S(1)}, bf16[2,2,5,32,1024]{4,3,2,1,0:T(8,128)(2,1)S(1)}) custom-call(s32[8]{0:T(128)S(1)} %copy-done.1, f32[1,256]{1,0:T(1,128)S(1)} %bitcast.2, bf16[4,4,32,256]{3,2,1,0:T(8,128)(2,1)S(1)} %copy-done, bf16[4,1,32,256]{3,2,1,0:T(8,128)(2,1)S(1)} %collective-permute-done.3.cross_ref, ...), custom_call_target="tpu_custom_call" | custom-call | bytes 8388608 | tf_op jit(solution)/shard_map/own/pallas_call | solution.py:301
  16.2 0.0 collective-permute-done.1.dcross_ref
  16.2 0.0 collective-permute-done.2.dchip_ref
  16.2 0.0 collective-permute-done.prev_ref
  16.3 0.0 copy-done.3
  16.3 11.7 %rest.1 = bf16[4,8,64,256]{3,2,1,0:T(8,128)(2,1)} custom-call(s32[8]{0:T(128)S(1)} %copy-done.1, f32[1,256]{1,0:T(1,128)S(1)} %bitcast.3, f32[1,256]{1,0:T(1,128)S(1)} %bitcast.4, bf16[4,4,32,256]{3,2,1,0:T(8,128)(2,1)S(1)} %collective-permute-done.prev_ref, bf16[4,1,32,256]{3,2,1,0:T(8,128)(2,1)S(1)} %collective-permute-done.1.dcross_ref, ...), custom_call_target="tpu_custom_call" | custom-call | flops 10737418240 | bytes 2097152 | tf_op jit(solution)/shard_map/rest/pallas_call | solution.py:314
Async XLA Ops:
  0.0 16.2 %collective-permute-start = (bf16[4,4,32,256]{3,2,1,0:T(8,128)(2,1)}, bf16[4,4,32,256]{3,2,1,0:T(8,128)(2,1)S(1)}, u32[]{:S(2)}, u32[]{:S(2)}) collective-permute-start(bf16[4,4,32,256]{3,2,1,0:T(8,128)(2,1)} %x_ref.1), channel_id=1, source_target_pairs={{0,8},{8,16},{16,24},{24,0},{1,9},{9,17},{17,25},{25,1},{2,10},{10... | collective-permute-start | bytes 786440 | tf_op jit(solution)/shard_map/ppermute | solution.py:18
  4.0 8.8 %collective-permute-start.3 = (bf16[4,1,32,256]{3,2,1,0:T(8,128)(2,1)S(1)}, bf16[4,1,32,256]{3,2,1,0:T(8,128)(2,1)S(1)}, u32[]{:S(2)}, u32[]{:S(2)}) collective-permute-start(bf16[4,1,32,256]{3,2,1,0:T(8,128)(2,1)S(1)} %get-tuple-element.11), channel_id=1, source_target_pairs={{0,7},{1,2},{2,1},{3,4},{4,3},{5,6},{6,5},{7,0},{8,15},{9,10},{10,... | collective-permute-start | bytes 196616 | tf_op jit(solution)/shard_map/ppermute | solution.py:280
  6.8 6.0 %copy-start = (bf16[4,4,32,256]{3,2,1,0:T(8,128)(2,1)S(1)}, bf16[4,4,32,256]{3,2,1,0:T(8,128)(2,1)}, u32[]{:S(2)}) copy-start(bf16[4,4,32,256]{3,2,1,0:T(8,128)(2,1)} %x_ref.1) | copy-start | bytes 786436
  6.8 6.0 %copy-start.1 = (s32[8]{0:T(128)S(1)}, s32[8]{0:T(128)}, u32[]{:S(2)}) copy-start(s32[8]{0:T(128)} %rows_ref.3) | copy-start | bytes 100
  6.8 6.1 %copy-start.2 = (f32[256]{0:T(256)S(1)}, f32[256]{0:T(256)}, u32[]{:S(2)}) copy-start(f32[256]{0:T(256)} %param.9) | copy-start | bytes 3076
  6.8 6.0 %collective-permute-start.4 = (bf16[4,1,32,256]{3,2,1,0:T(8,128)(2,1)S(1)}, bf16[4,1,32,256]{3,2,1,0:T(8,128)(2,1)S(1)}, u32[]{:S(2)}, u32[]{:S(2)}) collective-permute-start(bf16[4,1,32,256]{3,2,1,0:T(8,128)(2,1)S(1)} %get-tuple-element.12), channel_id=1, source_target_pairs={{0,1},{1,0},{2,3},{3,2},{4,5},{5,4},{6,7},{7,6},{8,9},{9,8},{10,11... | collective-permute-start | bytes 196616 | tf_op jit(solution)/shard_map/ppermute | solution.py:279
  6.8 9.4 %collective-permute-start.1 = (bf16[4,1,32,256]{3,2,1,0:T(8,128)(2,1)S(1)}, bf16[4,1,32,256]{3,2,1,0:T(8,128)(2,1)S(1)}, u32[]{:S(2)}, u32[]{:S(2)}) collective-permute-start(bf16[4,1,32,256]{3,2,1,0:T(8,128)(2,1)S(1)} %get-tuple-element.11), channel_id=1, source_target_pairs={{0,8},{1,10},{2,9},{3,12},{4,11},{5,14},{6,13},{7,15},{8,16},{9,18... | collective-permute-start | bytes 196616 | tf_op jit(solution)/shard_map/ppermute | solution.py:281
  8.3 7.9 %collective-permute-start.2 = (bf16[4,1,32,256]{3,2,1,0:T(8,128)(2,1)S(1)}, bf16[4,1,32,256]{3,2,1,0:T(8,128)(2,1)S(1)}, u32[]{:S(2)}, u32[]{:S(2)}) collective-permute-start(bf16[4,1,32,256]{3,2,1,0:T(8,128)(2,1)S(1)} %get-tuple-element.12), channel_id=1, source_target_pairs={{0,9},{1,8},{2,11},{3,10},{4,13},{5,12},{6,15},{7,14},{8,17},{9,16... | collective-permute-start | bytes 196616 | tf_op jit(solution)/shard_map/ppermute | solution.py:282
  12.8 3.5 %copy-start.3 = (f32[256]{0:T(256)S(1)}, f32[256]{0:T(256)}, u32[]{:S(2)}) copy-start(f32[256]{0:T(256)} %param.11) | copy-start | bytes 3076

commit v3 on v2

v3 whole, which is shorter than its diff:
```python
import functools

import jax
import jax.numpy as jnp
from jax import lax
from jax.experimental import pallas as pl
from jax.experimental.pallas import tpu as pltpu
from jax.sharding import PartitionSpec as P

F32 = jnp.float32
BF16 = jnp.bfloat16
AXES = ("tm", "tile")
FIRST_STEP = 2
CHUNK = 32


def rotated(block, axis):
    count = lax.axis_size(axis)
    return lax.ppermute(block, axis, [(i, (i + 1) % count) for i in range(count)])


def routes(groups, tiles, step, side):
    pairs = []
    for g in range(groups):
        for t in range(tiles):
            if side == "chip":
                to = t ^ 1
            else:
                to = t + 1 if t % 2 else t - 1
            if 0 <= to < tiles:
                pairs.append((g * tiles + t, ((g + step) % groups) * tiles + to))
            elif step:
                pairs.append((g * tiles + t, ((g + step) % groups) * tiles + t))
            else:
                pairs.append((g * tiles + t, g * tiles + tiles - 1 - t))
    return pairs


def down(v):
    n = v.shape[-2]
    ids = lax.broadcasted_iota(jnp.int32, v.shape, v.ndim - 2)
    return jnp.where(ids == 0, 0.0, pltpu.roll(v, 1, v.ndim - 2))


def up(v):
    n = v.shape[-2]
    ids = lax.broadcasted_iota(jnp.int32, v.shape, v.ndim - 2)
    return jnp.where(ids == n - 1, 0.0, pltpu.roll(v, n - 1, v.ndim - 2))


def pick_kernel(rows_hbm, x_hbm, _, __, cross_ref, chip_ref, rows_ref, x_ref, sem):
    copies = [
        pltpu.make_async_copy(rows_hbm, rows_ref, sem.at[0]),
        pltpu.make_async_copy(x_hbm, x_ref, sem.at[1]),
    ]
    for copy in copies:
        copy.start()
    for copy in copies:
        copy.wait()
    tile = lax.axis_index("tile")
    last = rows_ref[tile] - 1
    odd = lax.rem(tile, 2) == 1
    cross_ref[:, 0] = x_ref[:, jnp.where(odd, last, 0)]
    chip_ref[:, 0] = x_ref[:, jnp.where(odd, 0, last)]


def assemble(xs, own, cross_ref, chip_ref, chip_row, length, instead=None):
    frames, cap, cols, ch = own.shape
    tile = lax.axis_index("tile")
    odd = lax.rem(tile, 2) == 1
    has_cross = jnp.logical_and(tile > 0, tile < lax.axis_size("tile") - 1)
    for f in range(frames):
        cross = jnp.where(has_cross, cross_ref[f, 0], jnp.zeros((cols, ch), BF16))
        chip = chip_ref[f, chip_row]
        below = jnp.where(odd, cross, chip)
        rows = [jnp.where(odd, chip, cross), own[f, 0]]
        rows += [jnp.where(length == i, below, own[f, i]) for i in range(1, cap)] + [below]
        for i, z in enumerate(rows):
            if instead is not None:
                z = jnp.where(instead[0], instead[1][i], z)
            wide = z.astype(F32)
            xs[f, i, :, 0:ch] = down(wide).astype(BF16)
            xs[f, i, :, ch:2 * ch] = z
            xs[f, i, :, 2 * ch:3 * ch] = up(wide).astype(BF16)


def dot(lhs, rhs):
    return jnp.dot(lhs, rhs, preferred_element_type=F32)


def first_conv(sources, weights, bias, hs, f, length, beside):
    n = len(sources)
    _, _, half, cols, wide = hs.shape
    ch = wide // 4
    tile = lax.axis_index("tile")
    top = tile == 0
    bottom = tile == lax.axis_size("tile") - 1
    for phase in range(2):
        act = []
        for c in range(2):
            lhs = jnp.concatenate(
                [
                    jnp.concatenate(
                        [
                            ref[g, i:i + half, :, c * ch:(c + 2) * ch].reshape(half * cols, 2 * ch)
                            for a in range(3) for i in range(2) for ref, g in [taps[a]]
                        ],
                        axis=1,
                    )
                    for taps in sources
                ],
                axis=0,
            )
            v = dot(lhs, weights[phase][c].reshape(12 * ch, ch)) + bias
            for task in beside[2 * phase + c]:
                task()
            v = v / (1.0 + jnp.exp(-v))
            act.append(v.reshape(n, half, cols, ch))
        he, ho = act
        k = lax.broadcasted_iota(jnp.int32, he.shape, 1)
        if phase == 0:
            keep = jnp.logical_not(jnp.logical_and(bottom, k == length))
        else:
            keep = jnp.logical_not(jnp.logical_and(top, k == 0))
        he = jnp.where(keep, he, 0.0)
        ho = jnp.where(keep, ho, 0.0)
        for c, value in enumerate((down(ho) - ho, he + ho, ho - he, he - up(he))):
            hs[phase, f:f + n, :, :, c * ch:(c + 1) * ch] = value.astype(BF16)


def fold(k1_ref, w_ref, phase, a, rows):
    def pairs(x, y, z):
        return (x, y + z), (x + y, z)

    g = [[k1_ref[a, p, q, rows].astype(F32) for q in range(3)] for p in range(3)]
    by_row = [pairs(g[0][q], g[1][q], g[2][q])[phase] for q in range(3)]
    for i in range(2):
        taps = pairs(by_row[0][i], by_row[1][i], by_row[2][i])
        for c in range(2):
            for j in range(2):
                if i == phase and c == j:
                    w_ref[c, a, i, j, rows] = k1_ref[a, 2 * i, 2 * j, rows]
                else:
                    w_ref[c, a, i, j, rows] = taps[c][j].astype(BF16)


def fold_kernel(k1_ref, w_ref):
    parts = k1_ref.shape[3] // CHUNK

    def part(s, _):
        fold(k1_ref, w_ref, 0, s // parts, pl.ds(pl.multiple_of(lax.rem(s, parts) * CHUNK, CHUNK), CHUNK))
        return 0

    lax.fori_loop(0, 3 * parts, part, 0)


def spread(k2_ref, w2_ref, a, p, rows):
    x, y, z = (k2_ref[a, p, q, rows].astype(F32) * 0.5 for q in range(3))
    even = x + z
    w2_ref[0, a, p, rows] = (even + y).astype(BF16)
    w2_ref[1, a, p, rows] = (even - y).astype(BF16)


def own_kernel(rows_ref, b1_ref, x_ref, cross_ref, chip_ref, k1_ref, wa_ref, xs, hs, wb_ref):
    frames = x_ref.shape[0]
    length = rows_ref[lax.axis_index("tile")]
    assemble(xs, x_ref, cross_ref, chip_ref, 0, length)
    own = hs.shape[1]
    sources = [[(xs, frames - 2 - own + n + a) for a in range(3)] for n in range(own)]
    tasks = [
        functools.partial(fold, k1_ref, wb_ref, 1, a, slice(r, r + CHUNK))
        for a in range(3) for r in range(0, k1_ref.shape[3], CHUNK)
    ]
    first_conv(
        sources, (wa_ref, wb_ref), b1_ref[...], hs, 0, length, (tasks[0::2], tasks[1::2], (), ())
    )


def rest_kernel(
    rows_ref, b1_ref, b2_ref, prev_ref, dcross_ref, dchip_ref, xo, ho, wa_ref, wb_ref, k2_ref, out_hbm, xp, hp, w2_ref, mix, stage, sem
):
    frames, cap, cols, ch = prev_ref.shape
    tile = lax.axis_index("tile")
    length = rows_ref[tile]
    first = [xo[0, i, :, ch:2 * ch] for i in range(cap + 2)]
    assemble(xp, prev_ref, dcross_ref, dchip_ref, 0, length, (lax.axis_index("tm") == 0, first))

    tasks = [
        functools.partial(spread, k2_ref, w2_ref, a, p, slice(r, r + CHUNK))
        for a in range(3) for p in range(3) for r in range(0, k2_ref.shape[3], CHUNK)
    ]
    shared = hp.shape[1]
    source = [(xp, f) for f in range(frames)] + [(xo, f) for f in range(frames)]
    for f in range(0, shared, FIRST_STEP):
        first_conv(
            [[source[f + n + a] for a in range(3)] for n in range(FIRST_STEP)], (wa_ref, wb_ref), b1_ref[...], hp, f,
            length, [tasks[n::2 * shared] for n in range(2 * f, 2 * f + 4)],
        )

    bias_two = b2_ref[...]
    copies = []
    hidden = [(hp, f) for f in range(shared)] + [(ho, f) for f in range(ho.shape[1])]
    for r in range(2):
        rows = ((1, 0), (0, 0), (1, 1)) if r == 0 else ((0, 0), (1, 1), (0, 1))
        m = []
        for c in range(4):
            lhs = jnp.concatenate(
                [
                    jnp.concatenate(
                        [
                            ref[phase, g, k:k + cap, :, c * ch:(c + 1) * ch].reshape(cap * cols, ch)
                            for a in range(3) for phase, k in rows for ref, g in [hidden[f + a]]
                        ],
                        axis=1,
                    )
                    for f in range(frames)
                ],
                axis=0,
            )
            if c in (1, 2):
                taps = w2_ref[c - 1].reshape(9 * ch, ch)
            else:
                taps = jnp.concatenate([k2_ref[a, p, 2 * (c // 3)] for a in range(3) for p in range(3)], axis=0)
            m.append(dot(lhs, taps))
        sums = [
            (v + bias_two).reshape(frames, cap, cols, ch) for v in (m[0] + (m[1] + m[2]), (m[1] - m[2]) - m[3])
        ]
        for f in range(frames):
            for i in range(cap):
                residual = xo[f, i + 1, :, ch:2 * ch].astype(F32)
                keep = i < length
                for c in range(2):
                    value = jnp.where(keep, sums[c][f, i] + residual, 0.0)
                    for part in range(ch // 128):
                        mix[r, f, i, part, pl.ds(c, cols, stride=2), :] = value[:, 128 * part:128 * (part + 1)]
                for part in range(ch // 128):
                    lanes = slice(128 * part, 128 * (part + 1))
                    stage[r, f, i, :, lanes] = mix[r, f, i, part].astype(BF16)
            copies.append(pltpu.make_async_copy(stage.at[r, f], out_hbm.at[f, :, r], sem.at[r, f]))
            copies[-1].start()
    for copy in copies:
        copy.wait()


def in_hbm(value):
    return pltpu.with_memory_space_constraint(value, pltpu.HBM)


def in_vmem(value):
    return pltpu.with_memory_space_constraint(value, pltpu.VMEM)


def local(latent, tile_rows, kernel_one, bias_one, kernel_two, bias_two):
    frames, cap, cols, ch = latent.shape
    groups, tiles = lax.axis_size("tm"), lax.axis_size("tile")
    vmem = pl.BlockSpec(memory_space=pltpu.VMEM)
    smem = pl.BlockSpec(memory_space=pltpu.SMEM)
    hbm = pl.BlockSpec(memory_space=pltpu.HBM)
    bias_one, bias_two = bias_one.reshape(1, ch), bias_two.reshape(1, ch)

    prev = rotated(latent, "tm")
    rim = pltpu.VMEM((frames, 1, cols, ch), BF16)
    to_cross, to_chip = pl.pallas_call(
        pick_kernel,
        out_shape=(rim, rim),
        in_specs=[hbm] * 4,
        out_specs=(vmem, vmem),
        scratch_shapes=[
            pltpu.SMEM(tile_rows.shape, jnp.int32),
            pltpu.VMEM(latent.shape, BF16),
            pltpu.SemaphoreType.DMA((2,)),
        ],
        compiler_params=pltpu.CompilerParams(vmem_limit_bytes=4 << 20),
        cost_estimate=pl.CostEstimate(flops=0, bytes_accessed=1 << 19, transcendentals=0),
        name="pick",
    )(in_hbm(tile_rows), in_hbm(latent), in_hbm(kernel_one), in_hbm(kernel_two))
    chip = lax.ppermute(to_chip, AXES, routes(groups, tiles, 0, "chip"))
    cross = lax.ppermute(to_cross, AXES, routes(groups, tiles, 0, "cross"))
    dcross = lax.ppermute(to_cross, AXES, routes(groups, tiles, 1, "cross"))
    dchip = lax.ppermute(to_chip, AXES, routes(groups, tiles, 1, "chip"))

    kernel_one, kernel_two = in_vmem(kernel_one), in_vmem(kernel_two)
    folded = pltpu.VMEM((2, 3, 2, 2, ch, ch), BF16)
    wa = pl.pallas_call(
        fold_kernel,
        out_shape=folded,
        in_specs=[vmem],
        out_specs=vmem,
        compiler_params=pltpu.CompilerParams(vmem_limit_bytes=4 << 20),
        cost_estimate=pl.CostEstimate(flops=0, bytes_accessed=8 << 20, transcendentals=0),
        name="fold",
    )(kernel_one)
    wa = in_vmem(wa)

    own = frames - 2
    xo, ho, wb = pl.pallas_call(
        own_kernel,
        out_shape=(
            pltpu.VMEM((frames, cap + 2, cols, 3 * ch), BF16),
            pltpu.VMEM((2, own, cap + 1, cols, 4 * ch), BF16),
            folded,
        ),
        in_specs=[smem] + [vmem] * 6,
        out_specs=(vmem, vmem, vmem),
        compiler_params=pltpu.CompilerParams(vmem_limit_bytes=20 << 20),
        cost_estimate=pl.CostEstimate(flops=0, bytes_accessed=8 << 20, transcendentals=0),
        name="own",
    )(tile_rows, bias_one, latent, cross, chip, kernel_one, wa)

    mixed = pl.pallas_call(
        rest_kernel,
        out_shape=jax.ShapeDtypeStruct((frames, cap, 2, 2 * cols, ch), BF16),
        in_specs=[smem] + [vmem] * 10,
        out_specs=hbm,
        scratch_shapes=[
            pltpu.VMEM((frames, cap + 2, cols, 3 * ch), BF16),
            pltpu.VMEM((2, frames, cap + 1, cols, 4 * ch), BF16),
            pltpu.VMEM((2, 3, 3, ch, ch), BF16),
            pltpu.VMEM((2, frames, cap, ch // 128, 2 * cols, 128), F32),
            pltpu.VMEM((2, frames, cap, 2 * cols, ch), BF16),
            pltpu.SemaphoreType.DMA((2, frames)),
        ],
        compiler_params=pltpu.CompilerParams(vmem_limit_bytes=36 << 20),
        cost_estimate=pl.CostEstimate(flops=10 << 30, bytes_accessed=2 << 20, transcendentals=0),
        name="rest",
    )(
        tile_rows, bias_one, bias_two, prev, dcross, dchip,
        in_vmem(xo), in_vmem(ho), wa, in_vmem(wb), kernel_two,
    )
    return mixed.reshape(frames, 2 * cap, 2 * cols, ch)


def solution(mesh):
    in_specs = (P("tm", "tile", None, None), P(), P(), P(), P(), P())
    out_specs = P("tm", "tile", None, None)
    return jax.shard_map(local, mesh=mesh, in_specs=in_specs, out_specs=out_specs, check_vma=False)
```

time: 28.2 us -> 25.6 us (0.908)
  Pallas kernels: 19.4 us -> 16.3 us
  waiting for transfers between devices: 0.01 us -> 0.56 us
    pallas_call x3, Pallas kernels: 16.1 us -> 13 us  [the longest x1 11.2 us: local(): pl.pallas_call(rest_kernel, out_shape=jax.ShapeDtypeStruct((frames, cap,...]
    ppermute x1, waiting for transfers between devices: 0.01 us -> 0.55 us  [local(): dchip = lax.ppermute(to_chip, AXES, routes(groups, tiles, 1, 'chip'))]
  transfers between devices with their start and end apart: 5 -> 5, of which waited for: 0 -> 1; matrix products, arithmetic and copies ran while one was open for 0% -> 0% of each run, Pallas kernels for 28% -> 20%
where the time goes in v3:
time: 25.6 us; the launch traced here: 25.4 us
  Pallas kernels  16.3 us (64%)
  starting transfers between devices  8.4 us (33%)
  waiting for transfers between devices  0.56 us (2%)
    pallas_call x1, Pallas kernels, local(): pl.pallas_call(rest_kernel, out_shape=jax.ShapeDtypeStruct((frames, cap,...  11.2 us
    pallas_call x1, Pallas kernels, local(): pl.pallas_call(own_kernel, out_shape=(pltpu.VMEM((frames, cap + 2, cols,...  3.37 us
    ppermute x1, starting transfers between devices, rotated(): lax.ppermute(block, axis, [(i, (i + 1) % count) for i in range(count)])  2.94 us
    ppermute x1, starting transfers between devices, local(): cross = lax.ppermute(to_cross, AXES, routes(groups, tiles, 0, 'cross'))  2.83 us
    ppermute x1, starting transfers between devices, local(): dcross = lax.ppermute(to_cross, AXES, routes(groups, tiles, 1, 'cross'))  1.54 us
    ppermute x1, starting transfers between devices, local(): dchip = lax.ppermute(to_chip, AXES, routes(groups, tiles, 1, 'chip'))  1.09 us
    pallas_call x1, Pallas kernels, local(): pl.pallas_call(pick_kernel, out_shape=(rim, rim), in_specs=[hbm] * 4, out...  1.01 us
    pallas_call x1, Pallas kernels, local(): pl.pallas_call(fold_kernel, out_shape=folded, in_specs=[vmem], out_specs=...  0.75 us
  transfers between devices with their start and end apart: 5, of which 1 were waited for; matrix products, arithmetic and copies ran while one was open for 0% of the time, Pallas kernels for 20%

profile of v3, /device:TPU:0, one launch (start us, length us, event | category | flops | bytes accessed | tf_op | source)
XLA Modules:
  0.0 25.4 jit_solution(10453494976711171706)
XLA Ops:
  0.0 0.0 copy-start
  0.0 2.9 %collective-permute-start = (bf16[4,4,32,256]{3,2,1,0:T(8,128)(2,1)}, bf16[4,4,32,256]{3,2,1,0:T(8,128)(2,1)S(1)}, u32[]{:S(2)}, u32[]{:S(2)}) collective-permute-start(bf16[4,4,32,256]{3,2,1,0:T(8,128)(2,1)} %x_ref.1), channel_id=1, source_target_pairs={{0,8},{8,16},{16,24},{24,0},{1,9},{9,17},{17,25},{25,1},{2,10},{10... | collective-permute-start | bytes 786440 | tf_op jit(solution)/shard_map/ppermute | solution.py:19
  2.9 1.0 %pick.1 = (bf16[4,1,32,256]{3,2,1,0:T(8,128)(2,1)S(1)}, bf16[4,1,32,256]{3,2,1,0:T(8,128)(2,1)S(1)}) custom-call(s32[8]{0:T(128)} %rows_ref.3, bf16[4,4,32,256]{3,2,1,0:T(8,128)(2,1)} %x_ref.1, bf16[3,3,3,256,256]{4,3,2,1,0:T(8,128)(2,1)} %k1_ref.3, bf16[3,3,3,256,256]{4,3,2,1,0:T(8,128)(2,1)} %k2_ref.1), custom_call_target="tpu_custom_call" | custom-call | bytes 524288 | tf_op jit(solution)/shard_map/pick/pallas_call | solution.py:263
  4.0 2.8 %collective-permute-start.3 = (bf16[4,1,32,256]{3,2,1,0:T(8,128)(2,1)S(1)}, bf16[4,1,32,256]{3,2,1,0:T(8,128)(2,1)S(1)}, u32[]{:S(2)}, u32[]{:S(2)}) collective-permute-start(bf16[4,1,32,256]{3,2,1,0:T(8,128)(2,1)S(1)} %get-tuple-element.10), channel_id=1, source_target_pairs={{0,7},{1,2},{2,1},{3,4},{4,3},{5,6},{6,5},{7,0},{8,15},{9,10},{10,... | collective-permute-start | bytes 196616 | tf_op jit(solution)/shard_map/ppermute | solution.py:278
  6.8 0.0 copy-start.2
  6.8 0.0 collective-permute-start.4
  6.8 1.5 %collective-permute-start.1 = (bf16[4,1,32,256]{3,2,1,0:T(8,128)(2,1)S(1)}, bf16[4,1,32,256]{3,2,1,0:T(8,128)(2,1)S(1)}, u32[]{:S(2)}, u32[]{:S(2)}) collective-permute-start(bf16[4,1,32,256]{3,2,1,0:T(8,128)(2,1)S(1)} %get-tuple-element.10), channel_id=1, source_target_pairs={{0,8},{1,10},{2,9},{3,12},{4,11},{5,14},{6,13},{7,15},{8,16},{9,18... | collective-permute-start | bytes 196616 | tf_op jit(solution)/shard_map/ppermute | solution.py:279
  8.3 1.1 %collective-permute-start.2 = (bf16[4,1,32,256]{3,2,1,0:T(8,128)(2,1)S(1)}, bf16[4,1,32,256]{3,2,1,0:T(8,128)(2,1)S(1)}, u32[]{:S(2)}, u32[]{:S(2)}) collective-permute-start(bf16[4,1,32,256]{3,2,1,0:T(8,128)(2,1)S(1)} %get-tuple-element.11), channel_id=1, source_target_pairs={{0,9},{1,8},{2,11},{3,10},{4,13},{5,12},{6,15},{7,14},{8,17},{9,16... | collective-permute-start | bytes 196616 | tf_op jit(solution)/shard_map/ppermute | solution.py:280
  9.4 0.0 copy-done
  9.4 0.7 %fold.1.wa_ref = bf16[2,3,2,2,256,256]{5,4,3,2,1,0:T(8,128)(2,1)S(1)} custom-call(bf16[3,3,3,256,256]{4,3,2,1,0:T(8,128)(2,1)S(1)} %copy-done), custom_call_target="tpu_custom_call" | custom-call | bytes 8388608 | tf_op jit(solution)/shard_map/fold/pallas_call | solution.py:284
  10.2 0.0 collective-permute-done.3.cross_ref
  10.2 0.0 collective-permute-done.4.chip_ref
  10.2 0.0 copy-done.2
  10.2 0.0 copy-done.3
  10.2 0.0 copy-done.4
  10.2 0.0 copy-start.1
  10.3 0.0 copy-start.5
  10.3 3.4 %own.1 = (bf16[4,6,32,768]{3,2,1,0:T(8,128)(2,1)S(1)}, bf16[2,2,5,32,1024]{4,3,2,1,0:T(8,128)(2,1)S(1)}, bf16[2,3,2,2,256,256]{5,4,3,2,1,0:T(8,128)(2,1)S(1)}) custom-call(s32[8]{0:T(128)S(1)} %copy-done.3, f32[1,256]{1,0:T(1,128)S(1)} %bitcast.3, bf16[4,4,32,256]{3,2,1,0:T(8,128)(2,1)S(1)} %copy-done.2, ...), custom_call_target="tpu_custom_call" | custom-call | bytes 8388608 | tf_op jit(solution)/shard_map/own/pallas_call | solution.py:296
  13.6 0.0 collective-permute-done.1.dcross_ref
  13.7 0.5 %collective-permute-done.2.dchip_ref = bf16[4,1,32,256]{3,2,1,0:T(8,128)(2,1)S(1)} collective-permute-done((bf16[4,1,32,256]{3,2,1,0:T(8,128)(2,1)S(1)}, bf16[4,1,32,256]{3,2,1,0:T(8,128)(2,1)S(1)}, u32[]{:S(2)}, u32[]{:S(2)}) %collective-permute-start.2) | collective-permute-done | bytes 65568 | tf_op jit(solution)/shard_map/ppermute | solution.py:280
  14.2 0.0 collective-permute-done.prev_ref
  14.2 0.0 copy-done.1
  14.2 0.0 copy-done.5
  14.2 11.2 %rest.1 = bf16[4,4,2,64,256]{4,3,2,1,0:T(8,128)(2,1)} custom-call(s32[8]{0:T(128)S(1)} %copy-done.3, f32[1,256]{1,0:T(1,128)S(1)} %bitcast.4, f32[1,256]{1,0:T(1,128)S(1)} %bitcast.5, bf16[4,4,32,256]{3,2,1,0:T(8,128)(2,1)S(1)} %collective-permute-done.prev_ref, bf16[4,1,32,256]{3,2,1,0:T(8,128)(2,1)S(1)} %collective-permute-done.1.dcross_ref, ...), custom_call_target="tpu_custom_call" | custom-call | flops 10737418240 | bytes 2097152 | tf_op jit(solution)/shard_map/rest/pallas_call | solution.py:310
  (2 shorter events, 0.0 us)
Async XLA Ops:
  0.0 9.4 %copy-start = (bf16[3,3,3,256,256]{4,3,2,1,0:T(8,128)(2,1)S(1)}, bf16[3,3,3,256,256]{4,3,2,1,0:T(8,128)(2,1)}, u32[]{:S(2)}) copy-start(bf16[3,3,3,256,256]{4,3,2,1,0:T(8,128)(2,1)} %k1_ref.3) | copy-start | bytes 10616836
  0.0 14.2 %collective-permute-start = (bf16[4,4,32,256]{3,2,1,0:T(8,128)(2,1)}, bf16[4,4,32,256]{3,2,1,0:T(8,128)(2,1)S(1)}, u32[]{:S(2)}, u32[]{:S(2)}) collective-permute-start(bf16[4,4,32,256]{3,2,1,0:T(8,128)(2,1)} %x_ref.1), channel_id=1, source_target_pairs={{0,8},{8,16},{16,24},{24,0},{1,9},{9,17},{17,25},{25,1},{2,10},{10... | collective-permute-start | bytes 786440 | tf_op jit(solution)/shard_map/ppermute | solution.py:19
  4.0 6.2 %collective-permute-start.3 = (bf16[4,1,32,256]{3,2,1,0:T(8,128)(2,1)S(1)}, bf16[4,1,32,256]{3,2,1,0:T(8,128)(2,1)S(1)}, u32[]{:S(2)}, u32[]{:S(2)}) collective-permute-start(bf16[4,1,32,256]{3,2,1,0:T(8,128)(2,1)S(1)} %get-tuple-element.10), channel_id=1, source_target_pairs={{0,7},{1,2},{2,1},{3,4},{4,3},{5,6},{6,5},{7,0},{8,15},{9,10},{10,... | collective-permute-start | bytes 196616 | tf_op jit(solution)/shard_map/ppermute | solution.py:278
  6.8 3.4 %copy-start.2 = (bf16[4,4,32,256]{3,2,1,0:T(8,128)(2,1)S(1)}, bf16[4,4,32,256]{3,2,1,0:T(8,128)(2,1)}, u32[]{:S(2)}) copy-start(bf16[4,4,32,256]{3,2,1,0:T(8,128)(2,1)} %x_ref.1) | copy-start | bytes 786436
  6.8 3.4 %copy-start.3 = (s32[8]{0:T(128)S(1)}, s32[8]{0:T(128)}, u32[]{:S(2)}) copy-start(s32[8]{0:T(128)} %rows_ref.3) | copy-start | bytes 100
  6.8 3.4 %copy-start.4 = (f32[256]{0:T(256)S(1)}, f32[256]{0:T(256)}, u32[]{:S(2)}) copy-start(f32[256]{0:T(256)} %param.9) | copy-start | bytes 3076
  6.8 3.4 %collective-permute-start.4 = (bf16[4,1,32,256]{3,2,1,0:T(8,128)(2,1)S(1)}, bf16[4,1,32,256]{3,2,1,0:T(8,128)(2,1)S(1)}, u32[]{:S(2)}, u32[]{:S(2)}) collective-permute-start(bf16[4,1,32,256]{3,2,1,0:T(8,128)(2,1)S(1)} %get-tuple-element.11), channel_id=1, source_target_pairs={{0,1},{1,0},{2,3},{3,2},{4,5},{5,4},{6,7},{7,6},{8,9},{9,8},{10,11... | collective-permute-start | bytes 196616 | tf_op jit(solution)/shard_map/ppermute | solution.py:277
  6.8 6.8 %collective-permute-start.1 = (bf16[4,1,32,256]{3,2,1,0:T(8,128)(2,1)S(1)}, bf16[4,1,32,256]{3,2,1,0:T(8,128)(2,1)S(1)}, u32[]{:S(2)}, u32[]{:S(2)}) collective-permute-start(bf16[4,1,32,256]{3,2,1,0:T(8,128)(2,1)S(1)} %get-tuple-element.10), channel_id=1, source_target_pairs={{0,8},{1,10},{2,9},{3,12},{4,11},{5,14},{6,13},{7,15},{8,16},{9,18... | collective-permute-start | bytes 196616 | tf_op jit(solution)/shard_map/ppermute | solution.py:279
  8.3 5.9 %collective-permute-start.2 = (bf16[4,1,32,256]{3,2,1,0:T(8,128)(2,1)S(1)}, bf16[4,1,32,256]{3,2,1,0:T(8,128)(2,1)S(1)}, u32[]{:S(2)}, u32[]{:S(2)}) collective-permute-start(bf16[4,1,32,256]{3,2,1,0:T(8,128)(2,1)S(1)} %get-tuple-element.11), channel_id=1, source_target_pairs={{0,9},{1,8},{2,11},{3,10},{4,13},{5,12},{6,15},{7,14},{8,17},{9,16... | collective-permute-start | bytes 196616 | tf_op jit(solution)/shard_map/ppermute | solution.py:280
  10.2 4.0 %copy-start.1 = (bf16[3,3,3,256,256]{4,3,2,1,0:T(8,128)(2,1)S(1)}, bf16[3,3,3,256,256]{4,3,2,1,0:T(8,128)(2,1)}, u32[]{:S(2)}) copy-start(bf16[3,3,3,256,256]{4,3,2,1,0:T(8,128)(2,1)} %k2_ref.1) | copy-start | bytes 10616836
  10.3 4.0 %copy-start.5 = (f32[256]{0:T(256)S(1)}, f32[256]{0:T(256)}, u32[]{:S(2)}) copy-start(f32[256]{0:T(256)} %param.11) | copy-start | bytes 3076

commit v4 on v3

--- a/solution.py
+++ b/solution.py
@@ -29,8 +29,6 @@
                 to = t + 1 if t % 2 else t - 1
             if 0 <= to < tiles:
                 pairs.append((g * tiles + t, ((g + step) % groups) * tiles + to))
-            elif step:
-                pairs.append((g * tiles + t, ((g + step) % groups) * tiles + t))
             else:
                 pairs.append((g * tiles + t, g * tiles + tiles - 1 - t))
     return pairs

time: 25.6 us -> 25.1 us (0.980)
  waiting for transfers between devices: 0.56 us -> 0.01 us
    ppermute x1, waiting for transfers between devices: 0.55 us -> 0.01 us  [local(): dchip = lax.ppermute(to_chip, AXES, routes(groups, tiles, 1, 'chip'))]
    ppermute x1, starting transfers between devices: 1.09 us -> 1.58 us  [local(): dchip = lax.ppermute(to_chip, AXES, routes(groups, tiles, 1, 'chip'))]
    ppermute x1, starting transfers between devices: 1.54 us -> 1.06 us  [local(): dcross = lax.ppermute(to_cross, AXES, routes(groups, tiles, 1, 'cross'))]
  transfers between devices with their start and end apart: 5 -> 5, of which waited for: 1 -> 0; matrix products, arithmetic and copies ran while one was open for 0% -> 0% of each run, Pallas kernels for 20% -> 21%
where the time goes in v4:
time: 25.1 us; the launch traced here: 24.9 us
  Pallas kernels  16.3 us (65%)
  starting transfers between devices  8.4 us (33%)
    pallas_call x1, Pallas kernels, local(): pl.pallas_call(rest_kernel, out_shape=jax.ShapeDtypeStruct((frames, cap,...  11.2 us
    pallas_call x1, Pallas kernels, local(): pl.pallas_call(own_kernel, out_shape=(pltpu.VMEM((frames, cap + 2, cols,...  3.37 us
    ppermute x1, starting transfers between devices, rotated(): lax.ppermute(block, axis, [(i, (i + 1) % count) for i in range(count)])  2.94 us
    ppermute x1, starting transfers between devices, local(): cross = lax.ppermute(to_cross, AXES, routes(groups, tiles, 0, 'cross'))  2.83 us
    ppermute x1, starting transfers between devices, local(): dchip = lax.ppermute(to_chip, AXES, routes(groups, tiles, 1, 'chip'))  1.58 us
    ppermute x1, starting transfers between devices, local(): dcross = lax.ppermute(to_cross, AXES, routes(groups, tiles, 1, 'cross'))  1.06 us
    pallas_call x1, Pallas kernels, local(): pl.pallas_call(pick_kernel, out_shape=(rim, rim), in_specs=[hbm] * 4, out...  1.01 us
    pallas_call x1, Pallas kernels, local(): pl.pallas_call(fold_kernel, out_shape=folded, in_specs=[vmem], out_specs=...  0.75 us
  transfers between devices with their start and end apart: 5, of which 0 were waited for; matrix products, arithmetic and copies ran while one was open for 0% of the time, Pallas kernels for 21%

profile of v4, /device:TPU:0, one launch (start us, length us, event | category | flops | bytes accessed | tf_op | source)
XLA Modules:
  0.0 24.9 jit_solution(7565893027462606142)
XLA Ops:
  0.0 0.0 copy-start
  0.0 2.9 %collective-permute-start = (bf16[4,4,32,256]{3,2,1,0:T(8,128)(2,1)}, bf16[4,4,32,256]{3,2,1,0:T(8,128)(2,1)S(1)}, u32[]{:S(2)}, u32[]{:S(2)}) collective-permute-start(bf16[4,4,32,256]{3,2,1,0:T(8,128)(2,1)} %x_ref.1), channel_id=1, source_target_pairs={{0,8},{8,16},{16,24},{24,0},{1,9},{9,17},{17,25},{25,1},{2,10},{10... | collective-permute-start | bytes 786440 | tf_op jit(solution)/shard_map/ppermute | solution.py:19
  2.9 1.0 %pick.1 = (bf16[4,1,32,256]{3,2,1,0:T(8,128)(2,1)S(1)}, bf16[4,1,32,256]{3,2,1,0:T(8,128)(2,1)S(1)}) custom-call(s32[8]{0:T(128)} %rows_ref.3, bf16[4,4,32,256]{3,2,1,0:T(8,128)(2,1)} %x_ref.1, bf16[3,3,3,256,256]{4,3,2,1,0:T(8,128)(2,1)} %k1_ref.3, bf16[3,3,3,256,256]{4,3,2,1,0:T(8,128)(2,1)} %k2_ref.1), custom_call_target="tpu_custom_call" | custom-call | bytes 524288 | tf_op jit(solution)/shard_map/pick/pallas_call | solution.py:261
  4.0 2.8 %collective-permute-start.3 = (bf16[4,1,32,256]{3,2,1,0:T(8,128)(2,1)S(1)}, bf16[4,1,32,256]{3,2,1,0:T(8,128)(2,1)S(1)}, u32[]{:S(2)}, u32[]{:S(2)}) collective-permute-start(bf16[4,1,32,256]{3,2,1,0:T(8,128)(2,1)S(1)} %get-tuple-element.10), channel_id=1, source_target_pairs={{0,7},{1,2},{2,1},{3,4},{4,3},{5,6},{6,5},{7,0},{8,15},{9,10},{10,... | collective-permute-start | bytes 196616 | tf_op jit(solution)/shard_map/ppermute | solution.py:276
  6.8 0.0 copy-start.2
  6.8 0.0 collective-permute-start.4
  6.8 1.1 %collective-permute-start.1 = (bf16[4,1,32,256]{3,2,1,0:T(8,128)(2,1)S(1)}, bf16[4,1,32,256]{3,2,1,0:T(8,128)(2,1)S(1)}, u32[]{:S(2)}, u32[]{:S(2)}) collective-permute-start(bf16[4,1,32,256]{3,2,1,0:T(8,128)(2,1)S(1)} %get-tuple-element.10), channel_id=1, source_target_pairs={{0,7},{1,10},{2,9},{3,12},{4,11},{5,14},{6,13},{7,0},{8,15},{9,18}... | collective-permute-start | bytes 196616 | tf_op jit(solution)/shard_map/ppermute | solution.py:277
  7.9 1.6 %collective-permute-start.2 = (bf16[4,1,32,256]{3,2,1,0:T(8,128)(2,1)S(1)}, bf16[4,1,32,256]{3,2,1,0:T(8,128)(2,1)S(1)}, u32[]{:S(2)}, u32[]{:S(2)}) collective-permute-start(bf16[4,1,32,256]{3,2,1,0:T(8,128)(2,1)S(1)} %get-tuple-element.11), channel_id=1, source_target_pairs={{0,9},{1,8},{2,11},{3,10},{4,13},{5,12},{6,15},{7,14},{8,17},{9,16... | collective-permute-start | bytes 196616 | tf_op jit(solution)/shard_map/ppermute | solution.py:278
  9.4 0.0 copy-done
  9.4 0.7 %fold.1.wa_ref = bf16[2,3,2,2,256,256]{5,4,3,2,1,0:T(8,128)(2,1)S(1)} custom-call(bf16[3,3,3,256,256]{4,3,2,1,0:T(8,128)(2,1)S(1)} %copy-done), custom_call_target="tpu_custom_call" | custom-call | bytes 8388608 | tf_op jit(solution)/shard_map/fold/pallas_call | solution.py:282
  10.2 0.0 collective-permute-done.3.cross_ref
  10.2 0.0 collective-permute-done.4.chip_ref
  10.2 0.0 copy-done.2
  10.2 0.0 copy-done.3
  10.2 0.0 copy-done.4
  10.2 0.0 copy-start.1
  10.3 0.0 copy-start.5
  10.3 3.4 %own.1 = (bf16[4,6,32,768]{3,2,1,0:T(8,128)(2,1)S(1)}, bf16[2,2,5,32,1024]{4,3,2,1,0:T(8,128)(2,1)S(1)}, bf16[2,3,2,2,256,256]{5,4,3,2,1,0:T(8,128)(2,1)S(1)}) custom-call(s32[8]{0:T(128)S(1)} %copy-done.3, f32[1,256]{1,0:T(1,128)S(1)} %bitcast.3, bf16[4,4,32,256]{3,2,1,0:T(8,128)(2,1)S(1)} %copy-done.2, ...), custom_call_target="tpu_custom_call" | custom-call | bytes 8388608 | tf_op jit(solution)/shard_map/own/pallas_call | solution.py:294
  13.6 0.0 collective-permute-done.1.dcross_ref
  13.7 0.0 collective-permute-done.2.dchip_ref
  13.7 0.0 collective-permute-done.prev_ref
  13.7 0.0 copy-done.1
  13.7 0.0 copy-done.5
  13.7 11.2 %rest.1 = bf16[4,4,2,64,256]{4,3,2,1,0:T(8,128)(2,1)} custom-call(s32[8]{0:T(128)S(1)} %copy-done.3, f32[1,256]{1,0:T(1,128)S(1)} %bitcast.4, f32[1,256]{1,0:T(1,128)S(1)} %bitcast.5, bf16[4,4,32,256]{3,2,1,0:T(8,128)(2,1)S(1)} %collective-permute-done.prev_ref, bf16[4,1,32,256]{3,2,1,0:T(8,128)(2,1)S(1)} %collective-permute-done.1.dcross_ref, ...), custom_call_target="tpu_custom_call" | custom-call | flops 10737418240 | bytes 2097152 | tf_op jit(solution)/shard_map/rest/pallas_call | solution.py:308
  (2 shorter events, 0.0 us)
Async XLA Ops:
  0.0 9.4 %copy-start = (bf16[3,3,3,256,256]{4,3,2,1,0:T(8,128)(2,1)S(1)}, bf16[3,3,3,256,256]{4,3,2,1,0:T(8,128)(2,1)}, u32[]{:S(2)}) copy-start(bf16[3,3,3,256,256]{4,3,2,1,0:T(8,128)(2,1)} %k1_ref.3) | copy-start | bytes 10616836
  0.0 13.7 %collective-permute-start = (bf16[4,4,32,256]{3,2,1,0:T(8,128)(2,1)}, bf16[4,4,32,256]{3,2,1,0:T(8,128)(2,1)S(1)}, u32[]{:S(2)}, u32[]{:S(2)}) collective-permute-start(bf16[4,4,32,256]{3,2,1,0:T(8,128)(2,1)} %x_ref.1), channel_id=1, source_target_pairs={{0,8},{8,16},{16,24},{24,0},{1,9},{9,17},{17,25},{25,1},{2,10},{10... | collective-permute-start | bytes 786440 | tf_op jit(solution)/shard_map/ppermute | solution.py:19
  4.0 6.2 %collective-permute-start.3 = (bf16[4,1,32,256]{3,2,1,0:T(8,128)(2,1)S(1)}, bf16[4,1,32,256]{3,2,1,0:T(8,128)(2,1)S(1)}, u32[]{:S(2)}, u32[]{:S(2)}) collective-permute-start(bf16[4,1,32,256]{3,2,1,0:T(8,128)(2,1)S(1)} %get-tuple-element.10), channel_id=1, source_target_pairs={{0,7},{1,2},{2,1},{3,4},{4,3},{5,6},{6,5},{7,0},{8,15},{9,10},{10,... | collective-permute-start | bytes 196616 | tf_op jit(solution)/shard_map/ppermute | solution.py:276
  6.8 3.4 %copy-start.2 = (bf16[4,4,32,256]{3,2,1,0:T(8,128)(2,1)S(1)}, bf16[4,4,32,256]{3,2,1,0:T(8,128)(2,1)}, u32[]{:S(2)}) copy-start(bf16[4,4,32,256]{3,2,1,0:T(8,128)(2,1)} %x_ref.1) | copy-start | bytes 786436
  6.8 3.4 %copy-start.3 = (s32[8]{0:T(128)S(1)}, s32[8]{0:T(128)}, u32[]{:S(2)}) copy-start(s32[8]{0:T(128)} %rows_ref.3) | copy-start | bytes 100
  6.8 3.4 %copy-start.4 = (f32[256]{0:T(256)S(1)}, f32[256]{0:T(256)}, u32[]{:S(2)}) copy-start(f32[256]{0:T(256)} %param.9) | copy-start | bytes 3076
  6.8 3.4 %collective-permute-start.4 = (bf16[4,1,32,256]{3,2,1,0:T(8,128)(2,1)S(1)}, bf16[4,1,32,256]{3,2,1,0:T(8,128)(2,1)S(1)}, u32[]{:S(2)}, u32[]{:S(2)}) collective-permute-start(bf16[4,1,32,256]{3,2,1,0:T(8,128)(2,1)S(1)} %get-tuple-element.11), channel_id=1, source_target_pairs={{0,1},{1,0},{2,3},{3,2},{4,5},{5,4},{6,7},{7,6},{8,9},{9,8},{10,11... | collective-permute-start | bytes 196616 | tf_op jit(solution)/shard_map/ppermute | solution.py:275
  6.8 6.8 %collective-permute-start.1 = (bf16[4,1,32,256]{3,2,1,0:T(8,128)(2,1)S(1)}, bf16[4,1,32,256]{3,2,1,0:T(8,128)(2,1)S(1)}, u32[]{:S(2)}, u32[]{:S(2)}) collective-permute-start(bf16[4,1,32,256]{3,2,1,0:T(8,128)(2,1)S(1)} %get-tuple-element.10), channel_id=1, source_target_pairs={{0,7},{1,10},{2,9},{3,12},{4,11},{5,14},{6,13},{7,0},{8,15},{9,18}... | collective-permute-start | bytes 196616 | tf_op jit(solution)/shard_map/ppermute | solution.py:277
  7.9 5.8 %collective-permute-start.2 = (bf16[4,1,32,256]{3,2,1,0:T(8,128)(2,1)S(1)}, bf16[4,1,32,256]{3,2,1,0:T(8,128)(2,1)S(1)}, u32[]{:S(2)}, u32[]{:S(2)}) collective-permute-start(bf16[4,1,32,256]{3,2,1,0:T(8,128)(2,1)S(1)} %get-tuple-element.11), channel_id=1, source_target_pairs={{0,9},{1,8},{2,11},{3,10},{4,13},{5,12},{6,15},{7,14},{8,17},{9,16... | collective-permute-start | bytes 196616 | tf_op jit(solution)/shard_map/ppermute | solution.py:278
  10.2 3.4 %copy-start.1 = (bf16[3,3,3,256,256]{4,3,2,1,0:T(8,128)(2,1)S(1)}, bf16[3,3,3,256,256]{4,3,2,1,0:T(8,128)(2,1)}, u32[]{:S(2)}) copy-start(bf16[3,3,3,256,256]{4,3,2,1,0:T(8,128)(2,1)} %k2_ref.1) | copy-start | bytes 10616836
  10.3 3.4 %copy-start.5 = (f32[256]{0:T(256)S(1)}, f32[256]{0:T(256)}, u32[]{:S(2)}) copy-start(f32[256]{0:T(256)} %param.11) | copy-start | bytes 3076

commit v5 on v4

--- a/solution.py
+++ b/solution.py
@@ -62,12 +62,12 @@
     chip_ref[:, 0] = x_ref[:, jnp.where(odd, 0, last)]
 
 
-def assemble(xs, own, cross_ref, chip_ref, chip_row, length, instead=None):
-    frames, cap, cols, ch = own.shape
+def assemble(xs, own, cross_ref, chip_ref, chip_row, length, which, instead=None):
+    _, cap, cols, ch = own.shape
     tile = lax.axis_index("tile")
     odd = lax.rem(tile, 2) == 1
     has_cross = jnp.logical_and(tile > 0, tile < lax.axis_size("tile") - 1)
-    for f in range(frames):
+    for f in which:
         cross = jnp.where(has_cross, cross_ref[f, 0], jnp.zeros((cols, ch), BF16))
         chip = chip_ref[f, chip_row]
         below = jnp.where(odd, cross, chip)
@@ -162,7 +162,7 @@
 def own_kernel(rows_ref, b1_ref, x_ref, cross_ref, chip_ref, k1_ref, wa_ref, xs, hs, wb_ref):
     frames = x_ref.shape[0]
     length = rows_ref[lax.axis_index("tile")]
-    assemble(xs, x_ref, cross_ref, chip_ref, 0, length)
+    assemble(xs, x_ref, cross_ref, chip_ref, 0, length, range(frames))
     own = hs.shape[1]
     sources = [[(xs, frames - 2 - own + n + a) for a in range(3)] for n in range(own)]
     tasks = [
@@ -181,18 +181,22 @@
     tile = lax.axis_index("tile")
     length = rows_ref[tile]
     first = [xo[0, i, :, ch:2 * ch] for i in range(cap + 2)]
-    assemble(xp, prev_ref, dcross_ref, dchip_ref, 0, length, (lax.axis_index("tm") == 0, first))
-
+    earlier = functools.partial(assemble, xp, prev_ref, dcross_ref, dchip_ref, 0, length)
+    instead = (lax.axis_index("tm") == 0, first)
+    earlier(range(frames - FIRST_STEP, frames), instead)
     tasks = [
         functools.partial(spread, k2_ref, w2_ref, a, p, slice(r, r + CHUNK))
         for a in range(3) for p in range(3) for r in range(0, k2_ref.shape[3], CHUNK)
     ]
     shared = hp.shape[1]
     source = [(xp, f) for f in range(frames)] + [(xo, f) for f in range(frames)]
-    for f in range(0, shared, FIRST_STEP):
+    for f in reversed(range(0, shared, FIRST_STEP)):
+        beside = [tasks[n::2 * shared] for n in range(2 * f, 2 * f + 4)]
+        if f:
+            beside[0] = [functools.partial(earlier, range(f - FIRST_STEP, f), instead)] + beside[0]
         first_conv(
             [[source[f + n + a] for a in range(3)] for n in range(FIRST_STEP)], (wa_ref, wb_ref), b1_ref[...], hp, f,
-            length, [tasks[n::2 * shared] for n in range(2 * f, 2 * f + 4)],
+            length, beside,
         )
 
     bias_two = b2_ref[...]

time: 25.1 us -> 25.1 us (level)
  transfers between devices with their start and end apart: 5 -> 5, of which waited for: 0 -> 0; matrix products, arithmetic and copies ran while one was open for 0% -> 0% of each run, Pallas kernels for 21% -> 20%
where the time goes in v5:
time: 25.1 us; the launch traced here: 25 us
  Pallas kernels  16.4 us (65%)
  starting transfers between devices  8.4 us (33%)
    pallas_call x1, Pallas kernels, local(): pl.pallas_call(rest_kernel, out_shape=jax.ShapeDtypeStruct((frames, cap,...  11.3 us
    pallas_call x1, Pallas kernels, local(): pl.pallas_call(own_kernel, out_shape=(pltpu.VMEM((frames, cap + 2, cols,...  3.37 us
    ppermute x1, starting transfers between devices, rotated(): lax.ppermute(block, axis, [(i, (i + 1) % count) for i in range(count)])  2.94 us
    ppermute x1, starting transfers between devices, local(): cross = lax.ppermute(to_cross, AXES, routes(groups, tiles, 0, 'cross'))  2.83 us
    ppermute x1, starting transfers between devices, local(): dchip = lax.ppermute(to_chip, AXES, routes(groups, tiles, 1, 'chip'))  1.58 us
    ppermute x1, starting transfers between devices, local(): dcross = lax.ppermute(to_cross, AXES, routes(groups, tiles, 1, 'cross'))  1.06 us
    pallas_call x1, Pallas kernels, local(): pl.pallas_call(pick_kernel, out_shape=(rim, rim), in_specs=[hbm] * 4, out...  1.01 us
    pallas_call x1, Pallas kernels, local(): pl.pallas_call(fold_kernel, out_shape=folded, in_specs=[vmem], out_specs=...  0.75 us
  transfers between devices with their start and end apart: 5, of which 0 were waited for; matrix products, arithmetic and copies ran while one was open for 0% of the time, Pallas kernels for 20%

profile of v5, /device:TPU:0, one launch (start us, length us, event | category | flops | bytes accessed | tf_op | source)
XLA Modules:
  0.0 25.0 jit_solution(15532457384911990033)
XLA Ops:
  0.0 0.0 copy-start
  0.0 2.9 %collective-permute-start = (bf16[4,4,32,256]{3,2,1,0:T(8,128)(2,1)}, bf16[4,4,32,256]{3,2,1,0:T(8,128)(2,1)S(1)}, u32[]{:S(2)}, u32[]{:S(2)}) collective-permute-start(bf16[4,4,32,256]{3,2,1,0:T(8,128)(2,1)} %x_ref.1), channel_id=1, source_target_pairs={{0,8},{8,16},{16,24},{24,0},{1,9},{9,17},{17,25},{25,1},{2,10},{10... | collective-permute-start | bytes 786440 | tf_op jit(solution)/shard_map/ppermute | solution.py:19
  2.9 1.0 %pick.1 = (bf16[4,1,32,256]{3,2,1,0:T(8,128)(2,1)S(1)}, bf16[4,1,32,256]{3,2,1,0:T(8,128)(2,1)S(1)}) custom-call(s32[8]{0:T(128)} %rows_ref.3, bf16[4,4,32,256]{3,2,1,0:T(8,128)(2,1)} %x_ref.1, bf16[3,3,3,256,256]{4,3,2,1,0:T(8,128)(2,1)} %k1_ref.3, bf16[3,3,3,256,256]{4,3,2,1,0:T(8,128)(2,1)} %k2_ref.1), custom_call_target="tpu_custom_call" | custom-call | bytes 524288 | tf_op jit(solution)/shard_map/pick/pallas_call | solution.py:265
  4.0 2.8 %collective-permute-start.3 = (bf16[4,1,32,256]{3,2,1,0:T(8,128)(2,1)S(1)}, bf16[4,1,32,256]{3,2,1,0:T(8,128)(2,1)S(1)}, u32[]{:S(2)}, u32[]{:S(2)}) collective-permute-start(bf16[4,1,32,256]{3,2,1,0:T(8,128)(2,1)S(1)} %get-tuple-element.10), channel_id=1, source_target_pairs={{0,7},{1,2},{2,1},{3,4},{4,3},{5,6},{6,5},{7,0},{8,15},{9,10},{10,... | collective-permute-start | bytes 196616 | tf_op jit(solution)/shard_map/ppermute | solution.py:280
  6.8 0.0 copy-start.2
  6.8 0.0 collective-permute-start.4
  6.8 1.1 %collective-permute-start.1 = (bf16[4,1,32,256]{3,2,1,0:T(8,128)(2,1)S(1)}, bf16[4,1,32,256]{3,2,1,0:T(8,128)(2,1)S(1)}, u32[]{:S(2)}, u32[]{:S(2)}) collective-permute-start(bf16[4,1,32,256]{3,2,1,0:T(8,128)(2,1)S(1)} %get-tuple-element.10), channel_id=1, source_target_pairs={{0,7},{1,10},{2,9},{3,12},{4,11},{5,14},{6,13},{7,0},{8,15},{9,18}... | collective-permute-start | bytes 196616 | tf_op jit(solution)/shard_map/ppermute | solution.py:281
  7.9 1.6 %collective-permute-start.2 = (bf16[4,1,32,256]{3,2,1,0:T(8,128)(2,1)S(1)}, bf16[4,1,32,256]{3,2,1,0:T(8,128)(2,1)S(1)}, u32[]{:S(2)}, u32[]{:S(2)}) collective-permute-start(bf16[4,1,32,256]{3,2,1,0:T(8,128)(2,1)S(1)} %get-tuple-element.11), channel_id=1, source_target_pairs={{0,9},{1,8},{2,11},{3,10},{4,13},{5,12},{6,15},{7,14},{8,17},{9,16... | collective-permute-start | bytes 196616 | tf_op jit(solution)/shard_map/ppermute | solution.py:282
  9.4 0.0 copy-done
  9.4 0.7 %fold.1.wa_ref = bf16[2,3,2,2,256,256]{5,4,3,2,1,0:T(8,128)(2,1)S(1)} custom-call(bf16[3,3,3,256,256]{4,3,2,1,0:T(8,128)(2,1)S(1)} %copy-done), custom_call_target="tpu_custom_call" | custom-call | bytes 8388608 | tf_op jit(solution)/shard_map/fold/pallas_call | solution.py:286
  10.2 0.0 collective-permute-done.3.cross_ref
  10.2 0.0 collective-permute-done.4.chip_ref
  10.2 0.0 copy-done.2
  10.2 0.0 copy-done.3
  10.2 0.0 copy-done.4
  10.2 0.0 copy-start.1
  10.3 0.0 copy-start.5
  10.3 3.4 %own.1 = (bf16[4,6,32,768]{3,2,1,0:T(8,128)(2,1)S(1)}, bf16[2,2,5,32,1024]{4,3,2,1,0:T(8,128)(2,1)S(1)}, bf16[2,3,2,2,256,256]{5,4,3,2,1,0:T(8,128)(2,1)S(1)}) custom-call(s32[8]{0:T(128)S(1)} %copy-done.3, f32[1,256]{1,0:T(1,128)S(1)} %bitcast.3, bf16[4,4,32,256]{3,2,1,0:T(8,128)(2,1)S(1)} %copy-done.2, ...), custom_call_target="tpu_custom_call" | custom-call | bytes 8388608 | tf_op jit(solution)/shard_map/own/pallas_call | solution.py:298
  13.6 0.0 collective-permute-done.1.dcross_ref
  13.7 0.0 collective-permute-done.2.dchip_ref
  13.7 0.0 collective-permute-done.prev_ref
  13.7 0.0 copy-done.1
  13.7 0.0 copy-done.5
  13.7 11.3 %rest.1 = bf16[4,4,2,64,256]{4,3,2,1,0:T(8,128)(2,1)} custom-call(s32[8]{0:T(128)S(1)} %copy-done.3, f32[1,256]{1,0:T(1,128)S(1)} %bitcast.4, f32[1,256]{1,0:T(1,128)S(1)} %bitcast.5, bf16[4,4,32,256]{3,2,1,0:T(8,128)(2,1)S(1)} %collective-permute-done.prev_ref, bf16[4,1,32,256]{3,2,1,0:T(8,128)(2,1)S(1)} %collective-permute-done.1.dcross_ref, ...), custom_call_target="tpu_custom_call" | custom-call | flops 10737418240 | bytes 2097152 | tf_op jit(solution)/shard_map/rest/pallas_call | solution.py:312
  (2 shorter events, 0.0 us)
Async XLA Ops:
  0.0 9.4 %copy-start = (bf16[3,3,3,256,256]{4,3,2,1,0:T(8,128)(2,1)S(1)}, bf16[3,3,3,256,256]{4,3,2,1,0:T(8,128)(2,1)}, u32[]{:S(2)}) copy-start(bf16[3,3,3,256,256]{4,3,2,1,0:T(8,128)(2,1)} %k1_ref.3) | copy-start | bytes 10616836
  0.0 13.7 %collective-permute-start = (bf16[4,4,32,256]{3,2,1,0:T(8,128)(2,1)}, bf16[4,4,32,256]{3,2,1,0:T(8,128)(2,1)S(1)}, u32[]{:S(2)}, u32[]{:S(2)}) collective-permute-start(bf16[4,4,32,256]{3,2,1,0:T(8,128)(2,1)} %x_ref.1), channel_id=1, source_target_pairs={{0,8},{8,16},{16,24},{24,0},{1,9},{9,17},{17,25},{25,1},{2,10},{10... | collective-permute-start | bytes 786440 | tf_op jit(solution)/shard_map/ppermute | solution.py:19
  4.0 6.2 %collective-permute-start.3 = (bf16[4,1,32,256]{3,2,1,0:T(8,128)(2,1)S(1)}, bf16[4,1,32,256]{3,2,1,0:T(8,128)(2,1)S(1)}, u32[]{:S(2)}, u32[]{:S(2)}) collective-permute-start(bf16[4,1,32,256]{3,2,1,0:T(8,128)(2,1)S(1)} %get-tuple-element.10), channel_id=1, source_target_pairs={{0,7},{1,2},{2,1},{3,4},{4,3},{5,6},{6,5},{7,0},{8,15},{9,10},{10,... | collective-permute-start | bytes 196616 | tf_op jit(solution)/shard_map/ppermute | solution.py:280
  6.8 3.4 %copy-start.2 = (bf16[4,4,32,256]{3,2,1,0:T(8,128)(2,1)S(1)}, bf16[4,4,32,256]{3,2,1,0:T(8,128)(2,1)}, u32[]{:S(2)}) copy-start(bf16[4,4,32,256]{3,2,1,0:T(8,128)(2,1)} %x_ref.1) | copy-start | bytes 786436
  6.8 3.4 %copy-start.3 = (s32[8]{0:T(128)S(1)}, s32[8]{0:T(128)}, u32[]{:S(2)}) copy-start(s32[8]{0:T(128)} %rows_ref.3) | copy-start | bytes 100
  6.8 3.4 %copy-start.4 = (f32[256]{0:T(256)S(1)}, f32[256]{0:T(256)}, u32[]{:S(2)}) copy-start(f32[256]{0:T(256)} %param.9) | copy-start | bytes 3076
  6.8 3.4 %collective-permute-start.4 = (bf16[4,1,32,256]{3,2,1,0:T(8,128)(2,1)S(1)}, bf16[4,1,32,256]{3,2,1,0:T(8,128)(2,1)S(1)}, u32[]{:S(2)}, u32[]{:S(2)}) collective-permute-start(bf16[4,1,32,256]{3,2,1,0:T(8,128)(2,1)S(1)} %get-tuple-element.11), channel_id=1, source_target_pairs={{0,1},{1,0},{2,3},{3,2},{4,5},{5,4},{6,7},{7,6},{8,9},{9,8},{10,11... | collective-permute-start | bytes 196616 | tf_op jit(solution)/shard_map/ppermute | solution.py:279
  6.8 6.8 %collective-permute-start.1 = (bf16[4,1,32,256]{3,2,1,0:T(8,128)(2,1)S(1)}, bf16[4,1,32,256]{3,2,1,0:T(8,128)(2,1)S(1)}, u32[]{:S(2)}, u32[]{:S(2)}) collective-permute-start(bf16[4,1,32,256]{3,2,1,0:T(8,128)(2,1)S(1)} %get-tuple-element.10), channel_id=1, source_target_pairs={{0,7},{1,10},{2,9},{3,12},{4,11},{5,14},{6,13},{7,0},{8,15},{9,18}... | collective-permute-start | bytes 196616 | tf_op jit(solution)/shard_map/ppermute | solution.py:281
  7.9 5.8 %collective-permute-start.2 = (bf16[4,1,32,256]{3,2,1,0:T(8,128)(2,1)S(1)}, bf16[4,1,32,256]{3,2,1,0:T(8,128)(2,1)S(1)}, u32[]{:S(2)}, u32[]{:S(2)}) collective-permute-start(bf16[4,1,32,256]{3,2,1,0:T(8,128)(2,1)S(1)} %get-tuple-element.11), channel_id=1, source_target_pairs={{0,9},{1,8},{2,11},{3,10},{4,13},{5,12},{6,15},{7,14},{8,17},{9,16... | collective-permute-start | bytes 196616 | tf_op jit(solution)/shard_map/ppermute | solution.py:282
  10.2 3.4 %copy-start.1 = (bf16[3,3,3,256,256]{4,3,2,1,0:T(8,128)(2,1)S(1)}, bf16[3,3,3,256,256]{4,3,2,1,0:T(8,128)(2,1)}, u32[]{:S(2)}) copy-start(bf16[3,3,3,256,256]{4,3,2,1,0:T(8,128)(2,1)} %k2_ref.1) | copy-start | bytes 10616836
  10.3 3.4 %copy-start.5 = (f32[256]{0:T(256)S(1)}, f32[256]{0:T(256)}, u32[]{:S(2)}) copy-start(f32[256]{0:T(256)} %param.11) | copy-start | bytes 3076
